TPU v7x, 256 devices: a whole 4x4x8 slice. The times are simulated.
256 devices in a mesh: dp: 32 (over x, z_hi, core), mp: 8 (over y, z_lo).
Axes of the slice: x: 4, y: 4, z: 8 (z_hi: 4, z_lo: 2; z = z_hi * 2 + z_lo), core: 2. Of those that a mesh axis runs over, the one named last changes fastest.
Arguments:
- grads: bfloat16 [32, 48, 512, 512], P('dp', None, 'mp'), may hold values from -0.046875 to 0.046875
- owners: int32 [48, 1], replicated, may hold values from 0 to 31; in each aligned block of 48 rows (0 to 47, 48 to 95, ...) at most 4 rows name the same one
- left_stat: float32 [32, 4, 512, 512], P('dp', None, 'mp'), as said below
- right_stat: float32 [32, 4, 512, 512], P('dp', None, 'mp'), as said below
- first_moment: float32 [32, 4, 512, 512], P('dp', None, 'mp'), may hold values from -0.3 to 0.3
- second_moment: float32 [32, 4, 512, 512], P('dp', None, 'mp'), may hold values from 0.0001 to 0.01
Outputs:
- direction: bfloat16 [48, 512, 512], P(None, 'mp')
- left_out: float32 [32, 4, 512, 512], P('dp', None, 'mp')
- right_out: float32 [32, 4, 512, 512], P('dp', None, 'mp')
- first_out: float32 [32, 4, 512, 512], P('dp', None, 'mp')
- second_out: float32 [32, 4, 512, 512], P('dp', None, 'mp')
Inputs may be any that keep to these rules, and one draw needn't show every extreme that they name: `owners`: no owner holds more than 4 blocks, some owner holds exactly 4, and every owner holds at least one. `left_stat`: each slot's matrix is symmetric positive definite. `right_stat`: each slot's matrix is symmetric positive definite.
All inputs are finite; a program needn't handle non-finite values.
Results may differ from a plain program's by a relative error of at most 0.025.
Values may be sent and summed in bfloat16 or wider, within the bound.
A program may use at most 128 MiB of HBM per device.

v0:
```python
import jax
import jax.numpy as jnp
from jax import lax
from jax.sharding import Mesh
from jax.sharding import PartitionSpec as P

ITERS = 6
MP = ("mp_0", "mp_1")


def from_everyone(value, axis):
    copies = jnp.broadcast_to(value, (lax.axis_size(axis), *value.shape))
    return lax.all_to_all(copies, axis, split_axis=0, concat_axis=0, tiled=True)


def in_order(parts, dim):
    parts = jnp.moveaxis(parts, 0, dim)
    lengths = parts.shape
    return parts.reshape(*lengths[:dim], lengths[dim] * lengths[dim + 1], *lengths[dim + 2 :])


def gathered_copies(value, axis, dim):
    parts = from_everyone(value, axis)
    return in_order(parts, dim)


def gather_axes(value, axes, dim):
    for axis in reversed(axes):
        value = lax.all_gather(value, axis, axis=dim, tiled=True)
    return value


def multiply(left, right):
    return jnp.einsum("mik,mkj->mij", left, right, preferred_element_type=jnp.float32).astype(
        jnp.bfloat16
    )


def newton_roots(matrices):
    order_size = matrices.shape[-1]
    identity = jnp.eye(order_size, dtype=jnp.float32)
    frobenius = jnp.sqrt(jnp.sum(matrices * matrices, axis=(1, 2), keepdims=True))
    scaling = 5.0 / (2.0 * frobenius)
    current = (scaling * matrices).astype(jnp.bfloat16)
    root_now = (identity[None] * scaling**0.25).astype(jnp.bfloat16)
    for sweep in range(ITERS):
        factor_now = ((5.0 * identity[None] - current.astype(jnp.float32)) / 4.0).astype(
            jnp.bfloat16
        )
        root_now = multiply(root_now, factor_now)
        power_now = multiply(factor_now, factor_now)
        power_now = multiply(power_now, factor_now)
        power_now = multiply(power_now, factor_now)
        current = multiply(power_now, current)
    return root_now


def body(grads, owners, left_stat, right_stat, first_moment, second_moment):
    dp_count = lax.axis_size("dp")
    dp_index = lax.axis_index("dp")
    slot_count = left_stat.shape[1]
    block_count = grads.shape[1]
    row_count = grads.shape[2]
    owner_of = owners[:, 0]
    same_owner = (owner_of[:, None] == owner_of[None, :]).astype(jnp.int32)
    positions = jnp.arange(block_count, dtype=jnp.int32)
    earlier = (positions[None, :] < positions[:, None]).astype(jnp.int32)
    slot_of = jnp.sum(same_owner * earlier, axis=1)
    target = owner_of * slot_count + slot_of
    my_slots = dp_index * slot_count + jnp.arange(slot_count, dtype=jnp.int32)
    picker_int = (target[None, :] == my_slots[:, None]).astype(jnp.int32)
    occupied = jnp.sum(picker_int, axis=1) > 0
    all_slots = jnp.arange(dp_count * slot_count, dtype=jnp.int32)
    router = (target[None, :] == all_slots[:, None]).astype(jnp.bfloat16)
    send_buffer = jnp.einsum("gb,brc->grc", router, grads[0], preferred_element_type=jnp.float32)
    summed_grad = lax.psum_scatter(
        send_buffer.astype(jnp.bfloat16), "dp", scatter_dimension=0, tiled=True
    ).astype(jnp.float32)
    rounded = summed_grad.astype(jnp.bfloat16)
    full_grad = gathered_copies(rounded, MP, 1)
    row_start = lax.axis_index(MP) * row_count
    my_columns = lax.dynamic_slice_in_dim(full_grad, row_start, row_count, 2)
    left_term = jnp.einsum("sik,sjk->sij", rounded, full_grad, preferred_element_type=jnp.float32)
    right_term = jnp.einsum(
        "ski,skj->sij", my_columns, full_grad, preferred_element_type=jnp.float32
    )
    left_new = 0.9 * left_stat[0] + 0.1 * left_term
    right_new = 0.9 * right_stat[0] + 0.1 * right_term
    stacked = jnp.concatenate([left_new, right_new], axis=0)
    whole_stats = lax.all_to_all(stacked, MP, split_axis=0, concat_axis=1, tiled=True)
    my_roots = newton_roots(whole_stats)
    all_roots = gather_axes(my_roots, MP, 0)
    left_rows = lax.dynamic_slice_in_dim(all_roots[:slot_count], row_start, row_count, 1)
    left_half = jnp.einsum(
        "sik,skj->sij", left_rows, full_grad, preferred_element_type=jnp.float32
    ).astype(jnp.bfloat16)
    shampoo = jnp.einsum(
        "sik,skj->sij", left_half, all_roots[slot_count:], preferred_element_type=jnp.float32
    )
    first_new = 0.9 * first_moment[0] + 0.1 * summed_grad
    second_new = 0.95 * second_moment[0] + 0.05 * summed_grad * summed_grad
    adam_step = first_new / (jnp.sqrt(second_new) + 1e-08)
    adam_rows = jnp.sqrt(jnp.sum(adam_step * adam_step, axis=2, keepdims=True))
    shampoo_rows = jnp.sqrt(jnp.sum(shampoo * shampoo, axis=2, keepdims=True)) + 1e-06
    update_rows = (shampoo * (adam_rows / shampoo_rows)).astype(jnp.bfloat16)
    slot_mask = occupied[:, None, None]
    update_rows = jnp.where(slot_mask, update_rows, jnp.zeros_like(update_rows))
    collected = lax.all_gather(update_rows, "dp", axis=0, tiled=True)
    direction = jnp.take(collected, target, axis=0)
    left_out = jnp.where(slot_mask, left_new, left_stat[0])[None]
    right_out = jnp.where(slot_mask, right_new, right_stat[0])[None]
    first_out = jnp.where(slot_mask, first_new, first_moment[0])[None]
    second_out = jnp.where(slot_mask, second_new, second_moment[0])[None]
    return (direction, left_out, right_out, first_out, second_out)


def solution(mesh):
    finer = Mesh(mesh.devices.reshape(mesh.shape["dp"], 4, 2), ("dp", "mp_0", "mp_1"))
    in_specs = (
        P("dp", None, MP, None),
        P(),
        P("dp", None, MP, None),
        P("dp", None, MP, None),
        P("dp", None, MP, None),
        P("dp", None, MP, None),
    )
    out_specs = (
        P(None, MP, None),
        P("dp", None, MP, None),
        P("dp", None, MP, None),
        P("dp", None, MP, None),
        P("dp", None, MP, None),
    )
    return jax.shard_map(body, mesh=finer, in_specs=in_specs, out_specs=out_specs, check_vma=False)
```

profile of v0, /device:TPU:25, one launch (start us, length us, event | category | flops | bytes accessed | tf_op | source)
XLA Modules:
  0.0 435.4 jit_solution(13279394461547673024)
XLA Ops:
  9.1 8.3 %convolution_convert_fusion = bf16[128,64,512]{2,0,1:T(8,128)(2,1)} fusion(bf16[48,64,512]{2,1,0:T(8,128)(2,1)S(1)} %bitcast.94, s32[48]{0:T(128)S(1)} %multiply_add_fusion.1), kind=kOutput, calls=%fused_computation.1 | convolution fusion | flops 406853632 | bytes 11534528 | tf_op jit(solution)/shard_map/gb,brc->grc/dot_general | solution.py:75
  17.4 11.3 %copy.50 = bf16[128,64,512]{2,1,0:T(8,128)(2,1)} copy(bf16[128,64,512]{2,0,1:T(8,128)(2,1)} %convolution_convert_fusion) | data formatting | bytes 16777216 | tf_op jit(solution)/shard_map/convert_element_type | solution.py:77
  28.7 123.4 %reduce-scatter.2.cloned.1.call-done = bf16[4,64,512]{2,1,0:T(8,128)(2,1)} async-done(((bf16[128,64,512]{2,1,0:T(8,128)(2,1)}), bf16[4,64,512]{2,1,0:T(8,128)(2,1)}) %reduce-scatter.2.cloned.1.call-update) | async-done | bytes 262160 | tf_op jit(solution)/shard_map/reduce_scatter | solution.py:76
  154.6 4.3 all-to-all-start
  159.0 23.6 %all-to-all-done = bf16[8,4,64,512]{3,2,1,0:T(8,128)(2,1)} async-done(((bf16[8,4,64,512]{3,2,1,0:T(8,128)(2,1)}), bf16[8,4,64,512]{3,2,1,0:T(8,128)(2,1)}, u32[]{:S(2)}, u32[]{:S(2)}) %all-to-all-start) | async-done | bytes 2097184 | tf_op jit(solution)/shard_map/all_to_all | solution.py:13
  188.0 6.3 %all-to-all-start.1 = ((f32[8,64,512]{2,1,0:T(8,128)}), f32[8,64,512]{2,1,0:T(8,128)}, u32[]{:S(2)}, u32[]{:S(2)}) async-start(f32[8,64,512]{2,1,0:T(8,128)} %pad_maximum_fusion), calls=%async_computation.2 | async-start | bytes 2097152 | tf_op jit(solution)/shard_map/all_to_all | solution.py:90
  194.2 11.6 %all-to-all-done.1 = f32[8,64,512]{2,1,0:T(8,128)} async-done(((f32[8,64,512]{2,1,0:T(8,128)}), f32[8,64,512]{2,1,0:T(8,128)}, u32[]{:S(2)}, u32[]{:S(2)}) %all-to-all-start.1) | async-done | bytes 1048608 | tf_op jit(solution)/shard_map/all_to_all | solution.py:90
  211.2 3.1 convolution_convert_fusion.24
  217.2 3.0 convolution_convert_fusion.19
  225.8 3.3 convolution_convert_fusion.14
  229.2 3.0 convolution_convert_fusion.12
  232.1 3.2 convolution_convert_fusion.9
  235.3 2.9 convolution_convert_fusion.11
  238.2 3.0 convolution_convert_fusion.7
  241.2 3.3 convolution_convert_fusion.4
  244.5 3.0 fusion.5
  250.5 27.3 %all-gather.9.cloned.1.call-done = bf16[1024,512]{1,0:T(8,128)(2,1)} async-done(((bf16[512,512]{1,0:T(8,128)(2,1)}), bf16[1024,512]{1,0:T(8,128)(2,1)}) %all-gather.9.cloned.1.call-update) | async-done | bytes 1048592 | tf_op jit(solution)/shard_map/all_gather | solution.py:29
  278.0 3.7 fusion.26
  281.7 47.3 %all-gather.5.cloned.1.call-done = bf16[8,512,512]{2,1,0:T(8,128)(2,1)} async-done(((bf16[2,512,512]{2,1,0:T(8,128)(2,1)}), bf16[8,512,512]{2,1,0:T(8,128)(2,1)}) %all-gather.5.cloned.1.call-update) | async-done | bytes 4194320 | tf_op jit(solution)/shard_map/all_gather | solution.py:29
  329.1 3.1 slice.10
  332.1 4.0 multiply_reduce_fusion.1
  338.1 81.0 %all-gather.7.cloned.1.call-done = bf16[128,64,512]{2,1,0:T(8,128)(2,1)} async-done(((bf16[4,64,512]{2,1,0:T(8,128)(2,1)}), bf16[128,64,512]{2,1,0:T(8,128)(2,1)}) %all-gather.7.cloned.1.call-update) | async-done | bytes 8388624 | tf_op jit(solution)/shard_map/all_gather | solution.py:108
  419.0 5.9 %gather_fusion = bf16[48,64,512]{2,1,0:T(8,128)(2,1)} fusion(bf16[128,64,512]{2,1,0:T(8,128)(2,1)} %all-gather.7.cloned.1.call-done, s32[1024]{0:T(1024)S(1)} %pad_clamp_fusion), kind=kCustom, calls=%fused_computation | custom fusion | bytes 6291648 | tf_op jit(solution)/shard_map/jit(_take)/gather | solution.py:109
  424.9 3.9 broadcast_select_fusion
  (45 shorter events, 28.0 us)
Async XLA Ops:
  7.2 1.9 copy-start
  7.2 144.9 %reduce-scatter.2.cloned.1.call-start = ((), (), s32[]{:S(2)}) async-start(), calls=%async_computation.3 | async-start | bytes 8650752 | tf_op jit(solution)/shard_map/reduce_scatter | solution.py:76
  154.6 28.0 %all-to-all-start = ((bf16[8,4,64,512]{3,2,1,0:T(8,128)(2,1)}), bf16[8,4,64,512]{3,2,1,0:T(8,128)(2,1)}, u32[]{:S(2)}, u32[]{:S(2)}) async-start(bf16[8,4,64,512]{3,2,1,0:T(8,128)(2,1)} %broadcast_in_dim.70), calls=%async_computation.1 | async-start | bytes 4194304 | tf_op jit(solution)/shard_map/all_to_all | solution.py:13
  182.6 1.9 copy-start.5
  182.6 2.6 copy-start.4
  182.6 2.6 copy-start.6
  184.5 1.5 copy-start.1
  185.2 0.8 copy-start.2
  186.0 0.8 copy-start.3
  188.0 17.9 %all-to-all-start.1 = ((f32[8,64,512]{2,1,0:T(8,128)}), f32[8,64,512]{2,1,0:T(8,128)}, u32[]{:S(2)}, u32[]{:S(2)}) async-start(f32[8,64,512]{2,1,0:T(8,128)} %pad_maximum_fusion), calls=%async_computation.2 | async-start | bytes 2097152 | tf_op jit(solution)/shard_map/all_to_all | solution.py:90
  194.2 83.5 %all-gather.9.cloned.1.call-start = ((), (), s32[]{:S(2)}) async-start(), calls=%async_computation.6 | async-start | bytes 1572864 | tf_op jit(solution)/shard_map/all_gather | solution.py:29
  250.4 78.6 %all-gather.5.cloned.1.call-start = ((), (), s32[]{:S(2)}) async-start(), calls=%async_computation.4 | async-start | bytes 5242880 | tf_op jit(solution)/shard_map/all_gather | solution.py:29
  277.8 141.3 %all-gather.7.cloned.1.call-start = ((), (), s32[]{:S(2)}) async-start(), calls=%async_computation.5 | async-start | bytes 8650752 | tf_op jit(solution)/shard_map/all_gather | solution.py:108
  332.1 5.9 %copy-start.7 = (s32[48,1]{0,1:T(1,128)S(1)}, s32[48,1]{0,1:T(1,128)}, u32[]{:S(2)}) copy-start(s32[48,1]{0,1:T(1,128)} %param.7) | copy-start | bytes 580
Sparse Core Ops, SparseCore 0:
  28.8 123.2 reduce-scatter.1
  250.6 27.1 all-gather.8
  279.7 49.3 all-gather.4
  338.1 80.8 all-gather.6
where the time goes:
time: 437 us; the launch traced here: 435 us
  waiting for transfers between devices  314 us (72%)
  matrix products  52.9 us (12%)
  local copies, waits for them, and re-layouts  25.8 us (6%)
  other arithmetic  17.1 us (4%)
  between operations  14.7 us (3%)
  starting transfers between devices  10.7 us (2%)
    reduce_scatter x1, waiting for transfers between devices, body(): lax.psum_scatter(send_buffer.astype(jnp.bfloat16), 'dp', scatter_dimensio...  123 us
    all_gather x1, waiting for transfers between devices, body(): collected = lax.all_gather(update_rows, 'dp', axis=0, tiled=True)  81 us
    all_gather x2, waiting for transfers between devices, gather_axes(): value = lax.all_gather(value, axis, axis=dim, tiled=True)  74.6 us
    dot_general x13, matrix products, multiply(): jnp.einsum('mik,mkj->mij', left, right, preferred_element_type=jnp.float32)  39.2 us
    all_to_all x1, waiting for transfers between devices, from_everyone(): return lax.all_to_all(copies, axis, split_axis=0, concat_axis=0, tiled=True)  23.6 us
    all_to_all x1, waiting for transfers between devices, body(): lax.all_to_all(stacked, MP, split_axis=0, concat_axis=1, tiled=True)  11.6 us
    convert_element_type x1, local copies, waits for them, and re-layouts, body(): send_buffer.astype(jnp.bfloat16)  11.3 us
  transfers between devices with their start and end apart: 6, of which 6 were waited for; matrix products, arithmetic and copies ran while one was open for 1% of the time, Pallas kernels for 0%

commit v1 on v0

v1 whole, which is shorter than its diff:
```python
import jax
import jax.numpy as jnp
from jax import lax
from jax.experimental import pallas as pl
from jax.experimental.pallas import tpu as pltpu
from jax.sharding import PartitionSpec as P

ITERS = 6
MESH = pl.DeviceIdType.MESH
VMEM = pl.BlockSpec(memory_space=pltpu.VMEM)
SMEM = pl.BlockSpec(memory_space=pltpu.SMEM)
F32, BF16 = jnp.float32, jnp.bfloat16
NX, NZ, NC, NM = 4, 4, 2, 8
NK = NX * NZ
ROWS, COLS, HALF = 64, 512, 32
SLOTS = 4
BLOCKS = 48
OWNERS = NK * NC
EXTRAS = BLOCKS - OWNERS
FAR_FIRST = (2, 1, 3)


def place():
    me = lax.axis_index("dp")
    return me // (NZ * NC), (me // NC) % NZ, me % NC, lax.axis_index("mp")


def dp_of(x, z, c):
    return {"dp": (x * NZ + z) * NC + c}


def remote(src, dst, send, recv, device):
    copy = pltpu.make_async_remote_copy(
        src_ref=src, dst_ref=dst, send_sem=send, recv_sem=recv, device_id=device, device_id_type=MESH
    )
    copy.start()
    return copy


def greet(devices):
    barrier = pltpu.get_barrier_semaphore()
    for device in devices:
        pl.semaphore_signal(barrier, inc=1, device_id=device, device_id_type=MESH)
    pl.semaphore_wait(barrier, len(devices))


def dp_peers(x, z, c):
    return (
        [dp_of(x, z, 1 - c)]
        + [dp_of((x + k) % NX, z, c) for k in (1, 2, 3)]
        + [dp_of(x, (z + k) % NZ, c) for k in (1, 2, 3)]
    )


def mp_peers(j):
    return [{"mp": (j + k) % NM} for k in range(1, NM)]


def total(*parts):
    value = parts[0].astype(F32)
    for part in parts[1:]:
        value = value + part.astype(F32)
    return value.astype(BF16)


def spread_extras(ext, x, z, c, sz, rz, sx, rx, sc, rc):
    half = pl.ds(c * HALF, HALF)
    mine = ext.at[x * NZ + z, half]
    zs = [remote(mine, mine, sz.at[k - 1], rz.at[k - 1], dp_of(x, (z + k) % NZ, c)) for k in FAR_FIRST]
    for copy in zs:
        copy.wait_recv()
    line = ext.at[pl.ds(x * NZ, NZ), half]
    xs = [remote(line, line, sx.at[k - 1], rx.at[k - 1], dp_of((x + k) % NX, z, c)) for k in FAR_FIRST]
    cs = [remote(line, line, sc.at[0], rc.at[0], dp_of(x, z, 1 - c))]
    for k in (1, 3, 2):
        [copy] = [copy for copy, at in zip(xs, FAR_FIRST) if at == k]
        copy.wait_recv()
        came = ext.at[pl.ds(((x + NX - k) % NX) * NZ, NZ), half]
        cs.append(remote(came, came, sc.at[k], rc.at[k], dp_of(x, z, 1 - c)))
    return zs + xs, cs


def reduce_kernel(
    order, extra_of, grads, left_stat, right_stat, own, stat,
    send_f, send_e, recv_f, recv_e, acc_f, acc_e, from_x_f, from_z_f, from_x_e, from_z_e, sum_f, sum_e, ext,
    s_stat, r_stat, s_cf, r_cf, s_ce, r_ce, s_xf, r_xf, s_zf, r_zf, s_xe, r_xe, s_ze, r_ze,
    s_gz, r_gz, s_gx, r_gx, s_gc, r_gc,
):
    x, z, c, j = place()
    other = 1 - c
    greet(dp_peers(x, z, c) + mp_peers(j))

    for k in range(NK):
        send_e[k] = grads[order[OWNERS + k], pl.ds(other * HALF, HALF)]
    core_e = remote(send_e, recv_e, s_ce.at[0], r_ce.at[0], dp_of(x, z, other))
    core_f = []
    for step, k in enumerate((2, 1, 3, 0)):
        to = (x + k) % NX
        for q in range(NZ):
            send_f[to * NZ + q] = grads[order[(to * NZ + q) * NC + other]]
        rows = pl.ds(to * NZ, NZ)
        core_f.append(
            remote(send_f.at[rows], recv_f.at[rows], s_cf.at[step], r_cf.at[step], dp_of(x, z, other))
        )

    stat_rows = pl.ds(j * ROWS, ROWS)
    stats = []
    for k in range(1, NM):
        to = (j + k) % NM
        make = lambda source: pltpu.make_async_remote_copy(
            src_ref=source.at[to // 2], dst_ref=stat.at[stat_rows], send_sem=s_stat.at[k - 1],
            recv_sem=r_stat.at[k - 1], device_id={"mp": to}, device_id_type=MESH,
        )

        @pl.when(to % 2 == c)
        def _():
            make(left_stat).start()

        @pl.when(to % 2 != c)
        def _():
            make(right_stat).start()

        stats.append(make(left_stat))

    @pl.when(j % 2 == c)
    def _():
        stat[stat_rows] = left_stat[j // 2]

    @pl.when(j % 2 != c)
    def _():
        stat[stat_rows] = right_stat[j // 2]

    core_e.wait_recv()
    for k in range(NK):
        acc_e[k % NZ, k // NZ] = total(grads[order[OWNERS + k], pl.ds(c * HALF, HALF)], recv_e[k])
    z_e = []
    for k in FAR_FIRST:
        to = (z + k) % NZ
        z_e.append(remote(acc_e.at[to], from_z_e.at[k - 1], s_ze.at[k - 1], r_ze.at[k - 1], dp_of(x, to, c)))
    x_f = []
    for step, k in enumerate((2, 1, 3, 0)):
        to = (x + k) % NX
        core_f[step].wait_recv()
        for q in range(NZ):
            at = to * NZ + q
            acc_f[at] = total(grads[order[at * NC + c]], recv_f[at])
        if k:
            rows = pl.ds(to * NZ, NZ)
            x_f.append(
                remote(acc_f.at[rows], from_x_f.at[k - 1], s_xf.at[k - 1], r_xf.at[k - 1], dp_of(to, z, c))
            )
    for copy in z_e:
        copy.wait_recv()
    for q in range(NX):
        sum_e[q] = total(acc_e[z, q], from_z_e[0, q], from_z_e[1, q], from_z_e[2, q])
    x_e = []
    for k in FAR_FIRST:
        to = (x + k) % NX
        x_e.append(remote(sum_e.at[to], from_x_e.at[k - 1], s_xe.at[k - 1], r_xe.at[k - 1], dp_of(to, z, c)))
    for copy in x_f:
        copy.wait_recv()
    for q in range(NZ):
        sum_f[q] = total(acc_f[x * NZ + q], from_x_f[0, q], from_x_f[1, q], from_x_f[2, q])
    z_f = []
    for k in FAR_FIRST:
        to = (z + k) % NZ
        z_f.append(remote(sum_f.at[to], from_z_f.at[k - 1], s_zf.at[k - 1], r_zf.at[k - 1], dp_of(x, to, c)))
    for copy in x_e:
        copy.wait_recv()
    ext[x * NZ + z, pl.ds(c * HALF, HALF)] = total(sum_e[x], from_x_e[0], from_x_e[1], from_x_e[2])
    spread, cores = spread_extras(ext, x, z, c, s_gz, r_gz, s_gx, r_gx, s_gc, r_gc)
    for copy in z_f:
        copy.wait_recv()
    own[0] = total(sum_f[z], from_z_f[0], from_z_f[1], from_z_f[2])
    for copy in cores:
        copy.wait_recv()
    for s in range(1, SLOTS):
        own[s] = ext[extra_of[s]]
    for copy in stats:
        copy.wait()
    for copy in [core_e] + core_f + z_e + x_f + x_e + z_f + spread + cores:
        copy.wait_send()


def reduced(order, extra_of, grads, left_stat, right_stat):
    dma = pltpu.SemaphoreType.DMA
    pairs = [NM - 1, NX, 1, 3, 3, 3, 3, 3, 3, NX]
    return pl.pallas_call(
        reduce_kernel,
        out_shape=(
            jax.ShapeDtypeStruct((SLOTS, ROWS, COLS), BF16),
            jax.ShapeDtypeStruct((NM * ROWS, COLS), F32),
        ),
        in_specs=[SMEM, SMEM, VMEM, VMEM, VMEM],
        out_specs=(VMEM, VMEM),
        scratch_shapes=[
            pltpu.VMEM((NK, ROWS, COLS), BF16),
            pltpu.VMEM((NK, HALF, COLS), BF16),
            pltpu.VMEM((NK, ROWS, COLS), BF16),
            pltpu.VMEM((NK, HALF, COLS), BF16),
            pltpu.VMEM((NK, ROWS, COLS), BF16),
            pltpu.VMEM((NZ, NX, HALF, COLS), BF16),
            pltpu.VMEM((3, NZ, ROWS, COLS), BF16),
            pltpu.VMEM((3, ROWS, COLS), BF16),
            pltpu.VMEM((3, HALF, COLS), BF16),
            pltpu.VMEM((3, NX, HALF, COLS), BF16),
            pltpu.VMEM((NZ, ROWS, COLS), BF16),
            pltpu.VMEM((NX, HALF, COLS), BF16),
            pltpu.VMEM((EXTRAS, ROWS, COLS), BF16),
        ]
        + [dma((n,)) for n in pairs for _ in range(2)],
        compiler_params=pltpu.CompilerParams(
            collective_id=0, has_side_effects=True, vmem_limit_bytes=40 << 20
        ),
        name="reduce_grads",
    )(order, extra_of, grads, left_stat, right_stat)


def mm(a, b):
    return jnp.dot(a, b, preferred_element_type=F32)


def root_kernel(
    own, stat, first, second, terms, update,
    grad, norms, norms_in, mat, term, power, factor, current, root, half, half_in, turned,
    s_g, r_g, s_n, r_n, s_t, r_t, s_h, r_h, s_d, r_d,
):
    _, _, c, j = place()
    slot = j // 2
    side = (j + c) % 2
    partner = {"mp": j + 1 - 2 * (j % 2)}
    greet(mp_peers(j))
    my_rows = pl.ds(j * ROWS, ROWS)
    order = NM * ROWS

    g_copies = []
    for k in (4, 3, 5, 2, 6, 1, 7):
        to = (j + k) % NM
        g_copies.append(
            remote(own.at[to // 2], grad.at[my_rows], s_g.at[k - 1], r_g.at[k - 1], {"mp": to})
        )
    grad[my_rows] = own[slot]
    for s in range(SLOTS):
        g = own[s].astype(F32)
        m = 0.9 * first[s] + 0.1 * g
        v = 0.95 * second[s] + 0.05 * g * g
        a = m / (jnp.sqrt(v) + 1e-8)
        norms[s] = jnp.broadcast_to(jnp.sqrt(jnp.sum(a * a, axis=1, keepdims=True)), (ROWS, 128))
    norms_in[my_rows] = norms[slot]
    for copy in g_copies:
        copy.wait_recv()
    n_copies = []
    for k in range(1, NM):
        to = (j + k) % NM
        n_copies.append(
            remote(norms.at[to // 2], norms_in.at[my_rows], s_n.at[k - 1], r_n.at[k - 1], {"mp": to})
        )

    @pl.when(side == 0)
    def _():
        g = grad[...]
        mat[...] = lax.dot_general(g, g, (((1,), (1,)), ((), ())), preferred_element_type=F32)

    @pl.when(side == 1)
    def _():
        g = grad[...]
        mat[...] = lax.dot_general(g, g, (((0,), (0,)), ((), ())), preferred_element_type=F32)

    product = mat[...]
    term[...] = product.astype(BF16)
    whole = 0.9 * stat[...] + 0.1 * product
    mat[...] = whole
    t_copies = []
    for k in range(1, NM):
        to = (j + k) % NM
        t_copies.append(
            remote(
                term.at[pl.ds(to * ROWS, ROWS)], terms.at[side, slot], s_t.at[k - 1], r_t.at[j], {"mp": to}
            )
        )
    terms[side, slot] = term[my_rows]

    frobenius = jnp.sqrt(jnp.sum(whole * whole, keepdims=True))
    scaling = 5.0 / (2.0 * frobenius)
    start = jnp.sqrt(jnp.sqrt(scaling)).astype(BF16).astype(F32)
    diagonal = lax.broadcasted_iota(jnp.int32, (order, order), 0) == lax.broadcasted_iota(
        jnp.int32, (order, order), 1
    )
    five = jnp.where(diagonal, 5.0, 0.0).astype(F32)
    current[...] = (scaling * mat[...]).astype(BF16)
    factor[...] = ((five - current[...].astype(F32)) * 0.25).astype(BF16)
    root[...] = (start * factor[...].astype(F32)).astype(BF16)

    def sweep(_, carry):
        power[...] = mm(factor[...], factor[...]).astype(BF16)
        power[...] = mm(power[...], power[...]).astype(BF16)
        current[...] = mm(power[...], current[...]).astype(BF16)
        factor[...] = ((five - current[...].astype(F32)) * 0.25).astype(BF16)
        root[...] = mm(root[...], factor[...]).astype(BF16)
        return carry

    lax.fori_loop(0, ITERS - 1, sweep, 0)

    step = 2 * ROWS
    h_copies = []
    for i in range(order // step):
        rows = pl.ds(i * step, step)
        h_copies.append(
            pltpu.make_async_remote_copy(
                src_ref=half.at[rows], dst_ref=half_in.at[rows], send_sem=s_h.at[i], recv_sem=r_h.at[i],
                device_id=partner, device_id_type=MESH,
            )
        )
    d_copies = []
    for to in range(NM):
        d_copies.append(
            pltpu.make_async_remote_copy(
                src_ref=turned.at[pl.ds(to * ROWS, ROWS)], dst_ref=update.at[slot], send_sem=s_d.at[to],
                recv_sem=r_d.at[slot], device_id={"mp": to}, device_id_type=MESH,
            )
        )
    for k in range(1, NM):
        n_copies[k - 1].wait_recv()

    @pl.when(side == 0)
    def _():
        for i in range(order // step):
            rows = pl.ds(i * step, step)
            half[rows] = mm(root[rows], grad[...]).astype(BF16)
            h_copies[i].start()
        for copy in h_copies:
            copy.wait_send()

    @pl.when(side == 1)
    def _():
        for i in range(order // step):
            rows = pl.ds(i * step, step)
            h_copies[i].wait_recv()
            s = mm(half_in[rows], root[...])
            length = jnp.sqrt(jnp.sum(s * s, axis=1, keepdims=True)) + 1e-6
            turned[rows] = (s * (norms_in[rows, 0:1] / length)).astype(BF16)
            for to in (2 * i, 2 * i + 1):

                @pl.when(j != to)
                def _():
                    d_copies[to].start()

                @pl.when(j == to)
                def _():
                    update[slot] = turned[pl.ds(to * ROWS, ROWS)]

        for to in range(NM):

            @pl.when(j != to)
            def _():
                d_copies[to].wait_send()

    for s in range(SLOTS):

        @pl.when(j != 2 * s + 1 - c)
        def _():
            pltpu.make_async_remote_copy(
                src_ref=turned.at[pl.ds(0, ROWS)], dst_ref=update.at[s], send_sem=s_d.at[0],
                recv_sem=r_d.at[s], device_id=partner, device_id_type=MESH,
            ).wait_recv()

    for i in range(NM):

        @pl.when(j != i)
        def _():
            pltpu.make_async_remote_copy(
                src_ref=term.at[pl.ds(0, ROWS)], dst_ref=terms.at[(i + c) % 2, i // 2], send_sem=s_t.at[0],
                recv_sem=r_t.at[i], device_id=partner, device_id_type=MESH,
            ).wait_recv()

    for copy in g_copies + n_copies + t_copies:
        copy.wait_send()


def rooted(own, stat, first, second):
    dma = pltpu.SemaphoreType.DMA
    order = NM * ROWS
    square = lambda kind: pltpu.VMEM((order, COLS), kind)
    pairs = [NM - 1, NM - 1, None, order // (2 * ROWS), None]
    sems = [
        dma((NM - 1,)), dma((NM - 1,)), dma((NM - 1,)), dma((NM - 1,)), dma((NM - 1,)), dma((NM,)),
        dma((4,)), dma((4,)), dma((NM,)), dma((SLOTS,)),
    ]
    return pl.pallas_call(
        root_kernel,
        out_shape=(
            jax.ShapeDtypeStruct((2, SLOTS, ROWS, COLS), BF16),
            jax.ShapeDtypeStruct((SLOTS, ROWS, COLS), BF16),
        ),
        in_specs=[VMEM] * 4,
        out_specs=(VMEM, VMEM),
        scratch_shapes=[
            square(BF16),
            pltpu.VMEM((SLOTS, ROWS, 128), F32),
            pltpu.VMEM((order, 128), F32),
            square(F32),
        ]
        + [square(BF16)] * 8
        + sems,
        compiler_params=pltpu.CompilerParams(
            collective_id=1, has_side_effects=True, vmem_limit_bytes=40 << 20
        ),
        name="inverse_roots",
    )(own, stat, first, second)


def share_kernel(
    mine_of, place_of, update, out,
    all_of, send_e, recv_e, acc_e, from_x, from_z, sum_e,
    s_ce, r_ce, s_xe, r_xe, s_ze, r_ze, s_gz, r_gz, s_gx, r_gx, s_gc, r_gc, s_fz, r_fz, s_fx, r_fx, s_fc, r_fc,
):
    x, z, c, _ = place()
    other = 1 - c
    greet(dp_peers(x, z, c))
    me = c * NK + x * NZ + z
    all_of[me] = update[0]

    def picked(e, which):
        at = mine_of[e]
        kept = jnp.where(at > 0, 1.0, 0.0).astype(F32)
        value = update[at, pl.ds(which * HALF, HALF)].astype(F32)
        return jnp.where(jnp.full(value.shape, kept) > 0.5, value, 0.0)

    for e in range(EXTRAS):
        send_e[e] = picked(e, other).astype(BF16)
    core_e = remote(send_e, recv_e, s_ce.at[0], r_ce.at[0], dp_of(x, z, other))
    mine = all_of.at[me]
    f_z = [
        remote(mine, mine, s_fz.at[k - 1], r_fz.at[k - 1], dp_of(x, (z + k) % NZ, c)) for k in FAR_FIRST
    ]
    core_e.wait_recv()
    x_e = []
    for k in (2, 1, 3, 0):
        to = (x + k) % NX
        for q in range(NZ):
            e = to * NZ + q
            acc_e[e] = (picked(e, c) + recv_e[e].astype(F32)).astype(BF16)
        if k:
            rows = pl.ds(to * NZ, NZ)
            x_e.append(
                remote(acc_e.at[rows], from_x.at[k - 1], s_xe.at[k - 1], r_xe.at[k - 1], dp_of(to, z, c))
            )
    for copy in f_z:
        copy.wait_recv()
    line = all_of.at[pl.ds(c * NK + x * NZ, NZ)]
    f_x = [
        remote(line, line, s_fx.at[k - 1], r_fx.at[k - 1], dp_of((x + k) % NX, z, c)) for k in FAR_FIRST
    ]
    f_c = [remote(line, line, s_fc.at[0], r_fc.at[0], dp_of(x, z, other))]
    for copy in x_e:
        copy.wait_recv()
    for q in range(NZ):
        sum_e[q] = total(acc_e[x * NZ + q], from_x[0, q], from_x[1, q], from_x[2, q])
    z_e = []
    for k in FAR_FIRST:
        to = (z + k) % NZ
        z_e.append(remote(sum_e.at[to], from_z.at[k - 1], s_ze.at[k - 1], r_ze.at[k - 1], dp_of(x, to, c)))
    for copy in z_e:
        copy.wait_recv()
    all_of[OWNERS + x * NZ + z, pl.ds(c * HALF, HALF)] = total(sum_e[z], from_z[0], from_z[1], from_z[2])
    ext = all_of.at[pl.ds(OWNERS, EXTRAS)]
    spread, cores = spread_extras(ext, x, z, c, s_gz, r_gz, s_gx, r_gx, s_gc, r_gc)
    for k in (1, 3, 2):
        [copy] = [copy for copy, at in zip(f_x, FAR_FIRST) if at == k]
        copy.wait_recv()
        came = all_of.at[pl.ds(c * NK + ((x + NX - k) % NX) * NZ, NZ)]
        f_c.append(remote(came, came, s_fc.at[k], r_fc.at[k], dp_of(x, z, other)))
    for copy in f_c + cores:
        copy.wait_recv()
    for b in range(BLOCKS):
        out[b] = all_of[place_of[b]]
    for copy in [core_e] + f_z + x_e + f_x + z_e + spread + f_c + cores:
        copy.wait_send()


def shared(mine_of, place_of, update):
    dma = pltpu.SemaphoreType.DMA
    pairs = [1, 3, 3, 3, 3, NX, 3, 3, NX]
    return pl.pallas_call(
        share_kernel,
        out_shape=jax.ShapeDtypeStruct((BLOCKS, ROWS, COLS), BF16),
        in_specs=[SMEM, SMEM, VMEM],
        out_specs=VMEM,
        scratch_shapes=[
            pltpu.VMEM((BLOCKS, ROWS, COLS), BF16),
            pltpu.VMEM((EXTRAS, HALF, COLS), BF16),
            pltpu.VMEM((EXTRAS, HALF, COLS), BF16),
            pltpu.VMEM((EXTRAS, HALF, COLS), BF16),
            pltpu.VMEM((3, NZ, HALF, COLS), BF16),
            pltpu.VMEM((3, HALF, COLS), BF16),
            pltpu.VMEM((NZ, HALF, COLS), BF16),
        ]
        + [dma((n,)) for n in pairs for _ in range(2)],
        compiler_params=pltpu.CompilerParams(
            collective_id=2, has_side_effects=True, vmem_limit_bytes=40 << 20
        ),
        name="share_directions",
    )(mine_of, place_of, update)


def tables(owners):
    owner = owners[:, 0]
    me = lax.axis_index("dp")
    spots = jnp.arange(BLOCKS, dtype=jnp.int32)
    earlier = spots[None, :] < spots[:, None]
    slot = jnp.sum((owner[:, None] == owner[None, :]) & earlier, axis=1, dtype=jnp.int32)
    again = slot > 0
    rank = jnp.sum(again[None, :] & earlier, axis=1, dtype=jnp.int32)
    sorted_at = jnp.where(again, OWNERS + rank, owner)
    order = jnp.sum(jnp.where(sorted_at[None, :] == spots[:, None], spots[None, :], 0), axis=1)
    place_of = jnp.where(again, OWNERS + rank, (owner % NC) * NK + owner // NC)
    mine = owner == me
    slots = jnp.arange(SLOTS, dtype=jnp.int32)
    holds = mine[None, :] & (slot[None, :] == slots[:, None])
    occupied = jnp.any(holds, axis=1)
    extra_of = jnp.sum(jnp.where(holds & again[None, :], rank[None, :], 0), axis=1)
    extras = jnp.arange(EXTRAS, dtype=jnp.int32)
    held = (mine & again)[None, :] & (rank[None, :] == extras[:, None])
    mine_of = jnp.sum(jnp.where(held, slot[None, :], 0), axis=1)
    return order, place_of, occupied, extra_of, mine_of


def body(grads, owners, left_stat, right_stat, first_moment, second_moment):
    order, place_of, occupied, extra_of, mine_of = tables(owners)
    left, right, first, second = left_stat[0], right_stat[0], first_moment[0], second_moment[0]
    own, stat = reduced(order, extra_of, grads[0], left, right)
    terms, update = rooted(own, stat, first, second)
    direction = shared(mine_of, place_of, update)
    mask = occupied[:, None, None]
    summed = own.astype(F32)
    left_out = jnp.where(mask, 0.9 * left + 0.1 * terms[0].astype(F32), left)[None]
    right_out = jnp.where(mask, 0.9 * right + 0.1 * terms[1].astype(F32), right)[None]
    first_out = jnp.where(mask, 0.9 * first + 0.1 * summed, first)[None]
    second_out = jnp.where(mask, 0.95 * second + 0.05 * summed * summed, second)[None]
    return direction, left_out, right_out, first_out, second_out


def solution(mesh):
    split = P("dp", None, "mp", None)
    return jax.shard_map(
        body,
        mesh=mesh,
        in_specs=(split, P(), split, split, split, split),
        out_specs=(P(None, "mp", None), split, split, split, split),
        check_vma=False,
    )
```

time: 437 us -> 135 us (0.31)
  waiting for transfers between devices: 314 us -> 0 us
  Pallas kernels: 0 us -> 123 us
  matrix products: 52.9 us -> 0 us
  local copies, waits for them, and re-layouts: 25.8 us -> 5.66 us
  between operations: 14.7 us -> 0.72 us
  other arithmetic: 17.1 us -> 5.28 us
  starting transfers between devices: 10.7 us -> 0 us
    all_gather x3 -> x0, waiting for transfers between devices: 156 us -> none  [the longest x1 81 us: body(): collected = lax.all_gather(update_rows, 'dp', axis=0, tiled=True)]
    reduce_scatter x1 -> x0, waiting for transfers between devices: 123 us -> none  [body(): lax.psum_scatter(send_buffer.astype(jnp.bfloat16), 'dp', scatter_dimensio...]
    pallas_call x0 -> x3, Pallas kernels: none -> 123 us  [the longest x1 54.1 us: reduced(): pl.pallas_call(reduce_kernel, out_shape=(jax.ShapeDtypeStruct((SLOTS, ROW...]
    dot_general x17 -> x0, matrix products: 52.9 us -> none  [the longest x13 39.2 us: multiply(): jnp.einsum('mik,mkj->mij', left, right, preferred_element_type=jnp.float32)]
    all_to_all x2 -> x0, waiting for transfers between devices: 35.3 us -> none  [the longest x1 23.6 us: from_everyone(): return lax.all_to_all(copies, axis, split_axis=0, concat_axis=0, tiled=True)]
    convert_element_type x1 -> x0, local copies, waits for them, and re-layouts: 11.3 us -> none  [body(): send_buffer.astype(jnp.bfloat16)]
    all_to_all x2 -> x0, starting transfers between devices: 10.6 us -> none  [the longest x1 6.27 us: body(): lax.all_to_all(stacked, MP, split_axis=0, concat_axis=1, tiled=True)]
    gather x1 -> x0, local copies, waits for them, and re-layouts: 5.9 us -> none  [body(): direction = jnp.take(collected, target, axis=0)]
  transfers between devices with their start and end apart: 6 -> 0, of which waited for: 6 -> 0; matrix products, arithmetic and copies ran while one was open for 1% -> 0% of each run, Pallas kernels for 0% -> 0%
where the time goes in v1:
time: 135 us; the launch traced here: 134 us
  Pallas kernels  123 us (91%)
  local copies, waits for them, and re-layouts  5.66 us (4%)
  other arithmetic  5.28 us (4%)
    pallas_call x1, Pallas kernels, reduced(): pl.pallas_call(reduce_kernel, out_shape=(jax.ShapeDtypeStruct((SLOTS, ROW...  54.1 us
    pallas_call x1, Pallas kernels, shared(): pl.pallas_call(share_kernel, out_shape=jax.ShapeDtypeStruct((BLOCKS, ROWS...  36.8 us
    pallas_call x1, Pallas kernels, rooted(): pl.pallas_call(root_kernel, out_shape=(jax.ShapeDtypeStruct((2, SLOTS, RO...  31.8 us
    unnamed x15, local copies, waits for them, and re-layouts  5.66 us

profile of v1, /device:TPU:25, one launch (start us, length us, event | category | flops | bytes accessed | tf_op | source)
XLA Modules:
  0.0 134.3 jit_solution(14295120480819901784)
XLA Ops:
  0.6 0.9 convert_reduce_fusion.1
  1.5 0.7 fusion.14
  2.2 0.1 convert_reduce_fusion
  2.3 0.1 select_reduce_fusion.2.extra_of
  2.4 0.7 add_select_fusion.2
  3.1 0.1 select_reduce_fusion.order
  3.2 0.0 copy-start
  3.2 1.9 %copy-done = bf16[1,48,64,512]{3,2,1,0:T(8,128)(2,1)S(1)} copy-done((bf16[1,48,64,512]{3,2,1,0:T(8,128)(2,1)S(1)}, bf16[1,48,64,512]{3,2,1,0:T(8,128)(2,1)}, u32[]{:S(2)}) %copy-start) | copy-done | bytes 3145752
  5.1 1.0 copy-done.1
  6.2 1.0 copy-done.3
  7.2 54.1 %reduce_grads.1 = (bf16[4,64,512]{2,1,0:T(8,128)(2,1)S(1)}, f32[512,512]{1,0:T(8,128)S(1)}) custom-call(s32[48]{0:T(128)S(1)} %select_reduce_fusion.order, s32[4]{0:T(128)S(1)} %select_reduce_fusion.2.extra_of, bf16[48,64,512]{2,1,0:T(8,128)(2,1)S(1)} %bitcast.16, f32[4,64,512]{2,1,0:T(8,128)S(1)} %bitcast.17, f32[4,64,512]{2,1,0:T(8,128)S(1)} %bitcast.18), custom_call_target="tpu_custom_call" | custom-call | tf_op jit(solution)/shard_map/reduce_grads/pallas_call | solution.py:188
  61.3 0.0 copy-start.2
  61.3 0.0 copy-start.4
  61.3 0.0 copy-done.5
  61.3 0.0 copy-done.6
  61.3 31.8 %inverse_roots.1 = (bf16[2,4,64,512]{3,2,1,0:T(8,128)(2,1)S(1)}, bf16[4,64,512]{2,1,0:T(8,128)(2,1)S(1)}) custom-call(bf16[4,64,512]{2,1,0:T(8,128)(2,1)S(1)} %get-tuple-element.9.own, f32[512,512]{1,0:T(8,128)S(1)} %get-tuple-element.10.stat, f32[4,64,512]{2,1,0:T(8,128)S(1)} %bitcast.19, f32[4,64,512]{2,1,0:T(8,128)S(1)} %bitcast.20), custom_call_target="tpu_custom_call" | custom-call | tf_op jit(solution)/shard_map/inverse_roots/pallas_call | solution.py:389
  93.2 0.1 select_reduce_fusion.1.mine_of
  93.3 36.8 %share_directions.1 = bf16[48,64,512]{2,1,0:T(8,128)(2,1)S(1)} custom-call(s32[16]{0:T(128)S(1)} %select_reduce_fusion.1.mine_of, s32[48]{0:T(128)S(1)} %get-tuple-element.20.place_of, bf16[4,64,512]{2,1,0:T(8,128)(2,1)S(1)} %get-tuple-element.11.update), custom_call_target="tpu_custom_call" | custom-call | tf_op jit(solution)/shard_map/share_directions/pallas_call | solution.py:484
  130.1 0.1 fusion.10
  130.2 0.0 copy-done.2
  130.2 0.0 copy-done.4
  130.2 1.2 add_select_fusion
  131.4 1.2 fusion.5
  132.7 1.7 %copy.12 = bf16[48,64,512]{2,1,0:T(8,128)(2,1)} copy(bf16[48,64,512]{2,1,0:T(8,128)(2,1)S(1)} %share_directions.1) | data formatting | bytes 6291456
  (4 shorter events, 0.0 us)
Async XLA Ops:
  3.2 1.9 %copy-start = (bf16[1,48,64,512]{3,2,1,0:T(8,128)(2,1)S(1)}, bf16[1,48,64,512]{3,2,1,0:T(8,128)(2,1)}, u32[]{:S(2)}) copy-start(bf16[1,48,64,512]{3,2,1,0:T(8,128)(2,1)} %param.6) | copy-start | bytes 9437188
  5.1 1.0 copy-start.1
  6.2 1.0 copy-start.3
  7.2 54.1 %copy-start.5 = (f32[1,4,64,512]{3,2,1,0:T(8,128)S(1)}, f32[1,4,64,512]{3,2,1,0:T(8,128)}, u32[]{:S(2)}) copy-start(f32[1,4,64,512]{3,2,1,0:T(8,128)} %param.10) | copy-start | bytes 1572868
  7.2 54.1 %copy-start.6 = (f32[1,4,64,512]{3,2,1,0:T(8,128)S(1)}, f32[1,4,64,512]{3,2,1,0:T(8,128)}, u32[]{:S(2)}) copy-start(f32[1,4,64,512]{3,2,1,0:T(8,128)} %param.11) | copy-start | bytes 1572868
  61.3 68.9 %copy-start.2 = (f32[1,4,64,512]{3,2,1,0:T(8,128)S(1)}, f32[1,4,64,512]{3,2,1,0:T(8,128)}, u32[]{:S(2)}) copy-start(f32[1,4,64,512]{3,2,1,0:T(8,128)} %param.8) | copy-start | bytes 1572868
  61.3 68.9 %copy-start.4 = (f32[1,4,64,512]{3,2,1,0:T(8,128)S(1)}, f32[1,4,64,512]{3,2,1,0:T(8,128)}, u32[]{:S(2)}) copy-start(f32[1,4,64,512]{3,2,1,0:T(8,128)} %param.9) | copy-start | bytes 1572868

commit v2 on v0

v2 whole, which is shorter than its diff:
```python
import jax
import jax.numpy as jnp
from jax import lax
from jax.experimental import pallas as pl
from jax.experimental.pallas import tpu as pltpu
from jax.sharding import PartitionSpec as P

ITERS = 6
MESH = pl.DeviceIdType.MESH
VMEM = pl.BlockSpec(memory_space=pltpu.VMEM)
SMEM = pl.BlockSpec(memory_space=pltpu.SMEM)
ANY = pl.BlockSpec(memory_space=pl.ANY)
F32, BF16 = jnp.float32, jnp.bfloat16
NX, NZ, NC, NM = 4, 4, 2, 8
NK = NX * NZ
ROWS, COLS, HALF = 64, 512, 32
ORDER = NM * ROWS
SLOTS = 4
BLOCKS = 48
OWNERS = NK * NC
EXTRAS = BLOCKS - OWNERS
FAR_FIRST = (2, 1, 3)
SEMS = 192


def dp_of(x, z, c):
    return {"dp": (x * NZ + z) * NC + c}


def device_of(x, z, c, j):
    return {"dp": (x * NZ + z) * NC + c, "mp": j}


def total(*parts):
    value = parts[0].astype(F32)
    for part in parts[1:]:
        value = value + part.astype(F32)
    return value.astype(BF16)


def mm(a, b):
    return jnp.dot(a, b, preferred_element_type=F32)


class Wires:
    def __init__(self, send, recv):
        self.send, self.recv, self.used, self.sent = send, recv, 0, []

    def take(self, count):
        self.used += count
        assert self.used <= SEMS
        return self.used - count

    def make(self, src, dst, device, at_send, at_recv):
        return pltpu.make_async_remote_copy(
            src_ref=src, dst_ref=dst, send_sem=self.send.at[at_send], recv_sem=self.recv.at[at_recv],
            device_id=device, device_id_type=MESH,
        )

    def go(self, src, dst, device):
        at = self.take(1)
        copy = self.make(src, dst, device, at, at)
        copy.start()
        self.sent.append(copy)
        return copy


class RingReduce:
    def __init__(self, wires, acc, passed, came, x, to):
        self.wires, self.acc, self.passed, self.came, self.x, self.to = wires, acc, passed, came, x, to
        self.right, self.left, self.far = (x + 1) % NX, (x + 3) % NX, (x + 2) % NX

    def part(self, at, h):
        return self.acc.at[pl.ds(at * NZ + 2 * h, 2)]

    def send_far(self):
        self.a = self.wires.go(self.part(self.far, 0), self.passed.at[0], self.to(self.right))
        self.b = self.wires.go(self.part(self.far, 1), self.passed.at[1], self.to(self.left))

    def send_right(self):
        self.c = self.wires.go(self.part(self.right, 1), self.came.at[0, pl.ds(2, 2)], self.to(self.right))

    def send_left(self):
        self.d = self.wires.go(self.part(self.left, 0), self.came.at[1, pl.ds(0, 2)], self.to(self.left))

    def forward(self):
        self.a.wait_recv()
        for q in range(2):
            at = self.right * NZ + q
            self.acc[at] = total(self.acc[at], self.passed[0, q])
        self.e = self.wires.go(self.part(self.right, 0), self.came.at[0, pl.ds(0, 2)], self.to(self.right))
        self.b.wait_recv()
        for q in range(2):
            at = self.left * NZ + 2 + q
            self.acc[at] = total(self.acc[at], self.passed[1, q])
        self.f = self.wires.go(self.part(self.left, 1), self.came.at[1, pl.ds(2, 2)], self.to(self.left))

    def finish(self, out):
        for copy in (self.c, self.d, self.e, self.f):
            copy.wait_recv()
        for q in range(NZ):
            out[q] = total(self.acc[self.x * NZ + q], self.came[0, q], self.came[1, q])


class RingGather:
    def __init__(self, wires, part, x, to):
        self.wires, self.part = wires, part
        self.x, self.right, self.left = x, (x + 1) % NX, (x + 3) % NX
        self.to_right, self.to_left = to(self.right), to(self.left)

    def push(self, at, h, device):
        return self.wires.go(self.part(at, h), self.part(at, h), device)

    def start(self):
        self.a = self.push(self.x, 0, self.to_right)
        self.b = self.push(self.x, 1, self.to_left)
        self.c = self.push(self.x, 1, self.to_right)
        self.d = self.push(self.x, 0, self.to_left)

    def forward(self):
        self.a.wait_recv()
        self.e = self.push(self.left, 0, self.to_right)
        self.b.wait_recv()
        self.f = self.push(self.right, 1, self.to_left)

    def finish_near(self):
        self.c.wait_recv()
        self.d.wait_recv()

    def finish_far(self):
        self.e.wait_recv()
        self.f.wait_recv()


def kernel(
    order, place_of, occupied, extra_of, mine_of, grads, left, right, first, second,
    out, left_out, right_out, first_out, second_out,
    gv, lv, rv, fv, sv,
    send_f, send_e, recv_f, recv_e, acc_f, acc_e, pass_f, pass_e, came_f, came_e, sum_f, sum_e,
    from_z_f, from_z_e, ext, own,
    grad, stat, norms, norms_in, mat, term, terms, power, factor, current, root, half, half_in, turned, update,
    all_of, send_d, recv_d, acc_d, pass_d, came_d, sum_d, from_z_d,
    send_sem, recv_sem, load_sem, stat_sem,
):
    me = lax.axis_index("dp")
    j = lax.axis_index("mp")
    x, z, c = me // (NZ * NC), (me // NC) % NZ, me % NC
    y, zl = j // 2, j % 2
    other = 1 - c
    core = dp_of(x, z, other)
    to_x = lambda at: dp_of(at, z, c)
    w = Wires(send_sem, recv_sem)
    my_rows = pl.ds(j * ROWS, ROWS)
    lanes = lax.broadcasted_iota(jnp.int32, (ROWS, 128), 1)
    lines = lax.broadcasted_iota(jnp.int32, (ROWS, 128), 0)

    loads = [
        pltpu.make_async_copy(src, dst, load_sem.at[i])
        for i, (src, dst) in enumerate(((grads, gv), (left, lv), (right, rv), (first, fv), (second, sv)))
    ]
    for copy in loads:
        copy.start()

    barrier = pltpu.get_barrier_semaphore()
    greeted = 0
    for k in range(1, 4):
        for device in (dp_of((x + k) % NX, z, c), dp_of(x, (z + k) % NZ, c)):
            pl.semaphore_signal(barrier, inc=1, device_id=device, device_id_type=MESH)
            greeted += 1
    for k in range(NM):
        for which in range(NC):
            if k or which:
                device = device_of(x, z, (c + which) % NC, (j + k) % NM)
                pl.semaphore_signal(barrier, inc=1, device_id=device, device_id_type=MESH)
                greeted += 1
    pl.semaphore_wait(barrier, greeted)

    loads[0].wait()
    for k in range(NK):
        send_e[k] = gv[order[OWNERS + k], pl.ds(other * HALF, HALF)]
    core_e = w.go(send_e, recv_e, core)
    turns = (2, 1, 3, 0)
    core_f = []
    for k in turns:
        at = (x + k) % NX
        for q in range(NZ):
            send_f[at * NZ + q] = gv[order[(at * NZ + q) * NC + other]]
        rows = pl.ds(at * NZ, NZ)
        core_f.append(w.go(send_f.at[rows], recv_f.at[rows], core))

    loads[1].wait()
    loads[2].wait()
    stat_send, stat_recv = w.take(2 * SLOTS), w.take(NM)
    stat_copies = []
    for s in range(SLOTS):
        for role, source in enumerate((lv, rv)):
            copy = w.make(
                source.at[s], stat.at[my_rows], device_of(x, z, role, 2 * s + c), stat_send + 2 * s + role,
                stat_recv + j,
            )
            here = (c == role) & (j == 2 * s + c)
            stat_copies.append((here, copy))

            @pl.when(jnp.logical_not(here))
            def _():
                copy.start()

            @pl.when(here)
            def _():
                stat[my_rows] = source[s]

    ring_e = RingReduce(w, acc_e, pass_e, came_e, x, to_x)
    ring_f = RingReduce(w, acc_f, pass_f, came_f, x, to_x)
    core_e.wait_recv()
    for k in range(NK):
        acc_e[k] = total(gv[order[OWNERS + k], pl.ds(c * HALF, HALF)], recv_e[k])
    ring_e.send_far()
    ring_e.send_right()
    ring_e.send_left()

    def add_f(step):
        at = (x + turns[step]) % NX
        core_f[step].wait_recv()
        for q in range(NZ):
            acc_f[at * NZ + q] = total(gv[order[(at * NZ + q) * NC + c]], recv_f[at * NZ + q])

    add_f(0)
    ring_f.send_far()
    add_f(1)
    ring_f.send_right()
    ring_e.forward()
    add_f(2)
    ring_f.send_left()
    add_f(3)
    ring_e.finish(sum_e)
    z_e = [w.go(sum_e.at[(z + k) % NZ], from_z_e.at[k - 1], dp_of(x, (z + k) % NZ, c)) for k in FAR_FIRST]
    ring_f.forward()
    for copy in z_e:
        copy.wait_recv()
    mine = ext.at[x * NZ + z, pl.ds(c * HALF, HALF)]
    ext[x * NZ + z, pl.ds(c * HALF, HALF)] = total(sum_e[z], from_z_e[0], from_z_e[1], from_z_e[2])
    z_g = [w.go(mine, mine, dp_of(x, (z + k) % NZ, c)) for k in FAR_FIRST]
    ring_f.finish(sum_f)
    z_f = [w.go(sum_f.at[(z + k) % NZ], from_z_f.at[k - 1], dp_of(x, (z + k) % NZ, c)) for k in FAR_FIRST]
    for copy in z_g:
        copy.wait_recv()

    def spread(ref, base):
        part = lambda at, h: ref.at[pl.ds(base + at * NZ + 2 * h, 2), pl.ds(c * HALF, HALF)]
        line = lambda at: ref.at[pl.ds(base + at * NZ, NZ), pl.ds(c * HALF, HALF)]
        ring = RingGather(w, part, x, to_x)
        ring.start()
        across = [w.go(line(x), line(x), core)]
        ring.forward()
        ring.finish_near()
        for at in (ring.left, ring.right):
            across.append(w.go(line(at), line(at), core))
        ring.finish_far()
        far = (x + 2) % NX
        across.append(w.go(line(far), line(far), core))
        return across

    ext_core = spread(ext, 0)
    for copy in z_f:
        copy.wait_recv()
    own[0] = total(sum_f[z], from_z_f[0], from_z_f[1], from_z_f[2])

    g_send, g_recv, g_core = w.take(SLOTS), w.take(NM), w.take(NM)
    g_copies = [
        w.make(own.at[s], grad.at[my_rows], {"mp": 2 * s + c}, g_send + s, g_recv + j) for s in range(SLOTS)
    ]
    primary = c == zl

    def send_g(s):
        @pl.when(j != 2 * s + c)
        def _():
            g_copies[s].start()

        @pl.when(j == 2 * s + c)
        def _():
            grad[my_rows] = own[s]

    send_g(0)
    for copy in ext_core:
        copy.wait_recv()
    for s in range(1, SLOTS):
        own[s] = ext[extra_of[s]]
        send_g(s)

    loads[3].wait()
    loads[4].wait()
    n_send, n_recv = w.take(SLOTS), w.take(NM)
    n_copies = []
    for s in range(SLOTS):
        held = jnp.full((ROWS, COLS), occupied[s]) > 0
        g = own[s].astype(F32)
        m = 0.9 * fv[s] + 0.1 * g
        v = 0.95 * sv[s] + 0.05 * g * g
        first_out[s] = jnp.where(held, m, fv[s])
        second_out[s] = jnp.where(held, v, sv[s])
        a = m / (jnp.sqrt(v) + 1e-8)
        length = jnp.broadcast_to(jnp.sqrt(jnp.sum(a * a, axis=1, keepdims=True)), (ROWS, 128))
        length = jnp.sum(jnp.where(lanes == lines, length, 0.0), axis=0, keepdims=True)
        norms[s] = jnp.broadcast_to(length, (8, 128))
        copy = w.make(norms.at[s], norms_in.at[j], device_of(x, z, 1, 2 * s + c), n_send + s, n_recv + j)
        here = (c == 1) & (j == 2 * s + c)
        n_copies.append((here, copy))

        @pl.when(jnp.logical_not(here))
        def _():
            copy.start()

        @pl.when(here)
        def _():
            norms_in[j] = norms[s]

    handed = [
        w.make(grad.at[pl.ds(i * ROWS, ROWS)], grad.at[pl.ds(i * ROWS, ROWS)], core, g_core + i, g_core + i)
        for i in range(NM)
    ]

    @pl.when(primary)
    def _():
        for i in range(NM):

            @pl.when(j != i)
            def _():
                w.make(own.at[0], grad.at[pl.ds(i * ROWS, ROWS)], core, g_send, g_recv + i).wait_recv()

            handed[i].start()

    @pl.when(jnp.logical_not(primary))
    def _():
        for i in range(NM):
            handed[i].wait_recv()

    @pl.when(c == 0)
    def _():
        g = grad[...]
        mat[...] = lax.dot_general(g, g, (((1,), (1,)), ((), ())), preferred_element_type=F32)

    @pl.when(c == 1)
    def _():
        g = grad[...]
        mat[...] = lax.dot_general(g, g, (((0,), (0,)), ((), ())), preferred_element_type=F32)

    for i in range(NM):

        @pl.when(jnp.logical_not((zl == c) & (j == i)))
        def _():
            w.make(lv.at[0], stat.at[pl.ds(i * ROWS, ROWS)], core, stat_send, stat_recv + i).wait_recv()

    term[...] = mat[...].astype(BF16)
    t_send, t_recv = w.take(NM), w.take(2 * SLOTS)
    t_copies = []
    for i in range(NM):
        copy = w.make(
            term.at[pl.ds(i * ROWS, ROWS)], terms.at[c, y], device_of(x, z, zl, i), t_send + i,
            t_recv + c * SLOTS + y,
        )
        here = (zl == c) & (j == i)
        t_copies.append((here, copy))

        @pl.when(jnp.logical_not(here))
        def _():
            copy.start()

        @pl.when(here)
        def _():
            terms[c, y] = term[pl.ds(i * ROWS, ROWS)]

    whole = 0.9 * stat[...] + 0.1 * mat[...]
    mat[...] = whole
    frobenius = jnp.sqrt(jnp.sum(whole * whole, keepdims=True))
    scaling = 5.0 / (2.0 * frobenius)
    start = jnp.sqrt(jnp.sqrt(scaling)).astype(BF16).astype(F32)
    diagonal = lax.broadcasted_iota(jnp.int32, (ORDER, ORDER), 0) == lax.broadcasted_iota(
        jnp.int32, (ORDER, ORDER), 1
    )
    five = jnp.where(diagonal, 5.0, 0.0).astype(F32)
    current[...] = (scaling * mat[...]).astype(BF16)
    factor[...] = ((five - current[...].astype(F32)) * 0.25).astype(BF16)
    root[...] = (start * factor[...].astype(F32)).astype(BF16)

    def sweep(_, carry):
        power[...] = mm(factor[...], factor[...]).astype(BF16)
        power[...] = mm(power[...], power[...]).astype(BF16)
        current[...] = mm(power[...], current[...]).astype(BF16)
        factor[...] = ((five - current[...].astype(F32)) * 0.25).astype(BF16)
        root[...] = mm(root[...], factor[...]).astype(BF16)
        return carry

    lax.fori_loop(0, ITERS - 1, sweep, 0)

    step = 2 * ROWS
    count = ORDER // step
    h_at = w.take(count)
    h_copies = [
        w.make(half.at[pl.ds(i * step, step)], half_in.at[pl.ds(i * step, step)], core, h_at + i, h_at + i)
        for i in range(count)
    ]
    d_send, d_recv = w.take(NM), w.take(SLOTS)
    d_copies = [
        w.make(
            turned.at[pl.ds(i * ROWS, ROWS)], update.at[y], device_of(x, z, zl, i), d_send + i, d_recv + y
        )
        for i in range(NM)
    ]

    @pl.when(c == 0)
    def _():
        for i in range(count):
            rows = pl.ds(i * step, step)
            half[rows] = mm(root[rows], grad[...]).astype(BF16)
            h_copies[i].start()

    @pl.when(c == 1)
    def _():
        for i in range(NM):

            @pl.when(jnp.logical_not((zl == 1) & (j == i)))
            def _():
                w.make(norms.at[0], norms_in.at[i], core, n_send, n_recv + i).wait_recv()

        for i in range(count):
            rows = pl.ds(i * step, step)
            h_copies[i].wait_recv()
            s = mm(half_in[rows], root[...])
            for u in range(2):
                to = 2 * i + u
                here = (zl == 1) & (j == to)
                piece = s[u * ROWS : (u + 1) * ROWS]
                length = jnp.sqrt(jnp.sum(piece * piece, axis=1, keepdims=True)) + 1e-6
                adam = jnp.broadcast_to(norms_in[to, 0:1], (ROWS, 128))
                adam = jnp.sum(jnp.where(lanes == lines, adam, 0.0), axis=1, keepdims=True)
                turned[pl.ds(to * ROWS, ROWS)] = (piece * (adam / length)).astype(BF16)

                @pl.when(jnp.logical_not(here))
                def _():
                    d_copies[to].start()

                @pl.when(here)
                def _():
                    update[y] = turned[pl.ds(to * ROWS, ROWS)]

    def wait_update(s):
        @pl.when(jnp.logical_not((c == 1) & (j == 2 * s + c)))
        def _():
            w.make(turned.at[pl.ds(0, ROWS)], update.at[s], core, d_send, d_recv + s).wait_recv()

    here_f = c * NK + x * NZ + z
    wait_update(0)
    all_of[here_f] = update[0]
    f_z = [w.go(all_of.at[here_f], all_of.at[here_f], dp_of(x, (z + k) % NZ, c)) for k in FAR_FIRST]

    def ring_of(k):
        at_z = (z + NZ - k) % NZ
        part = lambda at, h: all_of.at[c * NK + at * NZ + at_z, pl.ds(h * HALF, HALF)]
        return RingGather(w, part, x, to_x)

    rings = {k: ring_of(k) for k in range(NZ)}
    rings[0].start()
    for s in range(1, SLOTS):
        wait_update(s)

    def picked(e, which):
        at = mine_of[e]
        value = update[at, pl.ds(which * HALF, HALF)]
        return jnp.where(jnp.full(value.shape, at) > 0, value.astype(F32), 0.0)

    for e in range(EXTRAS):
        send_d[e] = picked(e, other).astype(BF16)
    core_d = w.go(send_d, recv_d, core)
    core_d.wait_recv()
    ring_d = RingReduce(w, acc_d, pass_d, came_d, x, to_x)
    for k in turns:
        for q in range(NZ):
            e = ((x + k) % NX) * NZ + q
            acc_d[e] = (picked(e, c) + recv_d[e].astype(F32)).astype(BF16)
        if k == 2:
            ring_d.send_far()
        if k == 1:
            ring_d.send_right()
        if k == 3:
            ring_d.send_left()
    for copy, k in sorted(zip(f_z, FAR_FIRST), key=lambda pair: pair[1] == 2):
        copy.wait_recv()
        rings[k].start()
    f_line = lambda at: all_of.at[pl.ds(c * NK + at * NZ, NZ)]
    f_core = [w.go(f_line(x), f_line(x), core)]
    ring_d.forward()
    rings[0].forward()
    ring_d.finish(sum_d)
    z_d = [w.go(sum_d.at[(z + k) % NZ], from_z_d.at[k - 1], dp_of(x, (z + k) % NZ, c)) for k in FAR_FIRST]
    for k in (1, 3, 2):
        rings[k].forward()
    for copy in z_d:
        copy.wait_recv()
    here_e = (OWNERS + x * NZ + z, pl.ds(c * HALF, HALF))
    all_of[here_e] = total(sum_d[z], from_z_d[0], from_z_d[1], from_z_d[2])
    mine = all_of.at[here_e]
    z_g = [w.go(mine, mine, dp_of(x, (z + k) % NZ, c)) for k in FAR_FIRST]

    for role in range(2):
        for s in range(SLOTS):

            @pl.when(jnp.logical_not((role == c) & (j == 2 * s + c)))
            def _():
                w.make(
                    term.at[pl.ds(0, ROWS)], terms.at[role, s], core, t_send, t_recv + role * SLOTS + s
                ).wait_recv()

            old, new = ((lv, left_out), (rv, right_out))[role]
            held = jnp.full((ROWS, COLS), occupied[s]) > 0
            new[s] = jnp.where(held, 0.9 * old[s] + 0.1 * terms[role, s].astype(F32), old[s])

    for copy in z_g:
        copy.wait_recv()
    e_core = spread(all_of, OWNERS)
    for k in range(NZ):
        rings[k].finish_near()
    for at in ((x + 3) % NX, (x + 1) % NX):
        f_core.append(w.go(f_line(at), f_line(at), core))
    for k in range(NZ):
        rings[k].finish_far()
    f_core.append(w.go(f_line((x + 2) % NX), f_line((x + 2) % NX), core))
    for copy in f_core + e_core:
        copy.wait_recv()
    for b in range(BLOCKS):
        out[b] = all_of[place_of[b]]

    for copy in w.sent:
        copy.wait_send()
    for here, copy in stat_copies + n_copies + t_copies:

        @pl.when(jnp.logical_not(here))
        def _():
            copy.wait_send()

    for s in range(SLOTS):

        @pl.when(j != 2 * s + c)
        def _():
            g_copies[s].wait_send()

    @pl.when(primary)
    def _():
        for copy in handed:
            copy.wait_send()

    @pl.when(c == 0)
    def _():
        for copy in h_copies:
            copy.wait_send()

    @pl.when(c == 1)
    def _():
        for i in range(NM):

            @pl.when(jnp.logical_not((zl == 1) & (j == i)))
            def _():
                d_copies[i].wait_send()


def whole_step(order, place_of, occupied, extra_of, mine_of, grads, left, right, first, second):
    state = jax.ShapeDtypeStruct((SLOTS, ROWS, COLS), F32)
    v = lambda *shape, kind=BF16: pltpu.VMEM(shape, kind)
    dma = pltpu.SemaphoreType.DMA
    half = (HALF, COLS)
    full = (ROWS, COLS)
    return pl.pallas_call(
        kernel,
        out_shape=(jax.ShapeDtypeStruct((BLOCKS, ROWS, COLS), BF16), state, state, state, state),
        in_specs=[SMEM] * 5 + [ANY] * 5,
        out_specs=(VMEM,) * 5,
        scratch_shapes=[v(BLOCKS, *full)]
        + [v(SLOTS, *full, kind=F32)] * 4
        + [
            v(NK, *full), v(NK, *half), v(NK, *full), v(NK, *half), v(NK, *full), v(NK, *half),
            v(2, 2, *full), v(2, 2, *half), v(2, NZ, *full), v(2, NZ, *half), v(NZ, *full), v(NZ, *half),
            v(3, *full), v(3, *half), v(EXTRAS, *full), v(SLOTS, *full),
        ]
        + [
            v(ORDER, COLS), v(ORDER, COLS, kind=F32), v(SLOTS, 8, 128, kind=F32), v(NM, 8, 128, kind=F32),
            v(ORDER, COLS, kind=F32), v(ORDER, COLS), v(2, SLOTS, *full),
        ]
        + [v(ORDER, COLS)] * 7
        + [v(SLOTS, *full)]
        + [
            v(BLOCKS, *full), v(EXTRAS, *half), v(EXTRAS, *half), v(EXTRAS, *half), v(2, 2, *half),
            v(2, NZ, *half), v(NZ, *half), v(3, *half),
        ]
        + [dma((SEMS,)), dma((SEMS,)), dma((5,)), dma((1,))],
        compiler_params=pltpu.CompilerParams(
            collective_id=0, has_side_effects=True, vmem_limit_bytes=56 << 20
        ),
        name="shampoo_step",
    )(order, place_of, occupied, extra_of, mine_of, grads, left, right, first, second)


def tables(owners):
    owner = owners[:, 0]
    me = lax.axis_index("dp")
    spots = jnp.arange(BLOCKS, dtype=jnp.int32)
    earlier = spots[None, :] < spots[:, None]
    slot = jnp.sum((owner[:, None] == owner[None, :]) & earlier, axis=1, dtype=jnp.int32)
    again = slot > 0
    rank = jnp.sum(again[None, :] & earlier, axis=1, dtype=jnp.int32)
    sorted_at = jnp.where(again, OWNERS + rank, owner)
    order = jnp.sum(jnp.where(sorted_at[None, :] == spots[:, None], spots[None, :], 0), axis=1)
    place_of = jnp.where(again, OWNERS + rank, (owner % NC) * NK + owner // NC)
    mine = owner == me
    slots = jnp.arange(SLOTS, dtype=jnp.int32)
    holds = mine[None, :] & (slot[None, :] == slots[:, None])
    occupied = jnp.sum(holds, axis=1, dtype=jnp.int32)
    extra_of = jnp.sum(jnp.where(holds & again[None, :], rank[None, :], 0), axis=1)
    extras = jnp.arange(EXTRAS, dtype=jnp.int32)
    held = (mine & again)[None, :] & (rank[None, :] == extras[:, None])
    mine_of = jnp.sum(jnp.where(held, slot[None, :], 0), axis=1)
    return order, place_of, occupied, extra_of, mine_of


def body(grads, owners, left_stat, right_stat, first_moment, second_moment):
    direction, *states = whole_step(
        *tables(owners), grads[0], left_stat[0], right_stat[0], first_moment[0], second_moment[0]
    )
    return (direction, *(state[None] for state in states))


def solution(mesh):
    split = P("dp", None, "mp", None)
    return jax.shard_map(
        body,
        mesh=mesh,
        in_specs=(split, P(), split, split, split, split),
        out_specs=(P(None, "mp", None), split, split, split, split),
        check_vma=False,
    )
```

time: 437 us -> 123 us (0.28)
  waiting for transfers between devices: 314 us -> 0 us
  Pallas kernels: 0 us -> 108 us
  matrix products: 52.9 us -> 0 us
  local copies, waits for them, and re-layouts: 25.8 us -> 7.21 us
  between operations: 14.7 us -> 0.67 us
  other arithmetic: 17.1 us -> 4.8 us
  starting transfers between devices: 10.7 us -> 0 us
    all_gather x3 -> x0, waiting for transfers between devices: 156 us -> none  [the longest x1 81 us: body(): collected = lax.all_gather(update_rows, 'dp', axis=0, tiled=True)]
    reduce_scatter x1 -> x0, waiting for transfers between devices: 123 us -> none  [body(): lax.psum_scatter(send_buffer.astype(jnp.bfloat16), 'dp', scatter_dimensio...]
    pallas_call x0 -> x1, Pallas kernels: none -> 108 us  [whole_step(): pl.pallas_call(kernel, out_shape=(jax.ShapeDtypeStruct((BLOCKS, ROWS, COL...]
    dot_general x17 -> x0, matrix products: 52.9 us -> none  [the longest x13 39.2 us: multiply(): jnp.einsum('mik,mkj->mij', left, right, preferred_element_type=jnp.float32)]
    all_to_all x2 -> x0, waiting for transfers between devices: 35.3 us -> none  [the longest x1 23.6 us: from_everyone(): return lax.all_to_all(copies, axis, split_axis=0, concat_axis=0, tiled=True)]
    convert_element_type x1 -> x0, local copies, waits for them, and re-layouts: 11.3 us -> none  [body(): send_buffer.astype(jnp.bfloat16)]
    all_to_all x2 -> x0, starting transfers between devices: 10.6 us -> none  [the longest x1 6.27 us: body(): lax.all_to_all(stacked, MP, split_axis=0, concat_axis=1, tiled=True)]
    unnamed x16 -> x13, local copies, waits for them, and re-layouts: 1.09 us -> 7.21 us
  transfers between devices with their start and end apart: 6 -> 0, of which waited for: 6 -> 0; matrix products, arithmetic and copies ran while one was open for 1% -> 0% of each run, Pallas kernels for 0% -> 0%
where the time goes in v2:
time: 123 us; the launch traced here: 121 us
  Pallas kernels  108 us (88%)
  local copies, waits for them, and re-layouts  7.21 us (6%)
  other arithmetic  4.8 us (4%)
    pallas_call x1, Pallas kernels, whole_step(): pl.pallas_call(kernel, out_shape=(jax.ShapeDtypeStruct((BLOCKS, ROWS, COL...  108 us
    unnamed x13, local copies, waits for them, and re-layouts  7.21 us

profile of v2, /device:TPU:25, one launch (start us, length us, event | category | flops | bytes accessed | tf_op | source)
XLA Modules:
  0.0 121.1 jit_solution(1947549303099057085)
XLA Ops:
  0.6 0.9 convert_reduce_fusion.1
  1.5 0.7 fusion.7
  2.2 0.1 convert_reduce_fusion
  2.3 0.6 select_reduce_fusion.1.mine_of
  3.0 0.7 select_reduce_fusion.2
  3.6 1.2 fusion.6
  4.8 0.6 select_reduce_fusion.order
  5.4 108.4 %shampoo_step.1 = (bf16[48,64,512]{2,1,0:T(8,128)(2,1)}, f32[4,64,512]{2,1,0:T(8,128)}, f32[4,64,512]{2,1,0:T(8,128)}, f32[4,64,512]{2,1,0:T(8,128)}, f32[4,64,512]{2,1,0:T(8,128)}) custom-call(s32[48]{0:T(128)} %select_reduce_fusion.order, s32[48]{0:T(128)} %get-tuple-element.19.place_of, s32[4]{0:T(128)} %get-tuple-element.16.occupied, ...), custom_call_target="tpu_custom_call" | custom-call | tf_op jit(solution)/shard_map/shampoo_step/pallas_call | solution.py:571
  113.8 0.0 copy-start.3
  113.8 0.0 copy-start.2
  113.8 0.0 copy-start.1
  113.9 4.0 %copy.16 = bf16[48,64,512]{2,1,0:T(8,128)(2,1)} copy(bf16[48,64,512]{2,1,0:T(8,128)(2,1)} %get-tuple-element.27) | data formatting | bytes 6291456
  117.9 0.0 copy-done.3
  117.9 0.0 copy-start
  117.9 0.8 copy.17
  118.7 0.0 copy-done.2
  118.7 0.8 copy.18
  119.5 0.0 copy-done.1
  119.5 0.8 copy.19
  120.3 0.0 copy-done
  120.3 0.8 copy.20
Async XLA Ops:
  113.8 4.1 %copy-start.3 = (f32[4,64,512]{2,1,0:T(8,128)S(1)}, f32[4,64,512]{2,1,0:T(8,128)}, u32[]{:S(2)}) copy-start(f32[4,64,512]{2,1,0:T(8,128)} %get-tuple-element.11) | copy-start | bytes 1572868
  113.8 4.8 %copy-start.2 = (f32[4,64,512]{2,1,0:T(8,128)S(1)}, f32[4,64,512]{2,1,0:T(8,128)}, u32[]{:S(2)}) copy-start(f32[4,64,512]{2,1,0:T(8,128)} %get-tuple-element.12) | copy-start | bytes 1572868
  113.8 5.6 %copy-start.1 = (f32[4,64,512]{2,1,0:T(8,128)S(1)}, f32[4,64,512]{2,1,0:T(8,128)}, u32[]{:S(2)}) copy-start(f32[4,64,512]{2,1,0:T(8,128)} %get-tuple-element.13) | copy-start | bytes 1572868
  117.9 2.4 %copy-start = (f32[4,64,512]{2,1,0:T(8,128)S(1)}, f32[4,64,512]{2,1,0:T(8,128)}, u32[]{:S(2)}) copy-start(f32[4,64,512]{2,1,0:T(8,128)} %get-tuple-element.14) | copy-start | bytes 1572868

commit v3 on v2

--- a/solution.py
+++ b/solution.py
@@ -21,6 +21,7 @@
 EXTRAS = BLOCKS - OWNERS
 FAR_FIRST = (2, 1, 3)
 SEMS = 192
+PLACE_OF, OCCUPIED, EXTRA_OF, MINE_OF, TABLE = 48, 96, 100, 104, 128
 
 
 def dp_of(x, z, c):
@@ -133,14 +134,14 @@
 
 
 def kernel(
-    order, place_of, occupied, extra_of, mine_of, grads, left, right, first, second,
-    out, left_out, right_out, first_out, second_out,
-    gv, lv, rv, fv, sv,
+    table, grads, left, right, first, second,
+    all_out, left_hbm, right_hbm, first_hbm, second_hbm,
+    gv, lv, rv, fv, sv, all_of, left_out, right_out, first_out, second_out,
     send_f, send_e, recv_f, recv_e, acc_f, acc_e, pass_f, pass_e, came_f, came_e, sum_f, sum_e,
     from_z_f, from_z_e, ext, own,
     grad, stat, norms, norms_in, mat, term, terms, power, factor, current, root, half, half_in, turned, update,
-    all_of, send_d, recv_d, acc_d, pass_d, came_d, sum_d, from_z_d,
-    send_sem, recv_sem, load_sem, stat_sem,
+    send_d, recv_d, acc_d, pass_d, came_d, sum_d, from_z_d,
+    send_sem, recv_sem, load_sem, store_sem,
 ):
     me = lax.axis_index("dp")
     j = lax.axis_index("mp")
@@ -177,16 +178,33 @@
 
     loads[0].wait()
     for k in range(NK):
-        send_e[k] = gv[order[OWNERS + k], pl.ds(other * HALF, HALF)]
+        send_e[k] = gv[table[OWNERS + k], pl.ds(other * HALF, HALF)]
     core_e = w.go(send_e, recv_e, core)
     turns = (2, 1, 3, 0)
     core_f = []
     for k in turns:
         at = (x + k) % NX
         for q in range(NZ):
-            send_f[at * NZ + q] = gv[order[(at * NZ + q) * NC + other]]
+            send_f[at * NZ + q] = gv[table[(at * NZ + q) * NC + other]]
         rows = pl.ds(at * NZ, NZ)
         core_f.append(w.go(send_f.at[rows], recv_f.at[rows], core))
+
+    ring_e = RingReduce(w, acc_e, pass_e, came_e, x, to_x)
+    ring_f = RingReduce(w, acc_f, pass_f, came_f, x, to_x)
+    core_e.wait_recv()
+
+    def add_e(step):
+        for q in range(NZ):
+            k = ((x + turns[step]) % NX) * NZ + q
+            acc_e[k] = total(gv[table[OWNERS + k], pl.ds(c * HALF, HALF)], recv_e[k])
+
+    add_e(0)
+    ring_e.send_far()
+    add_e(1)
+    ring_e.send_right()
+    add_e(2)
+    ring_e.send_left()
+    add_e(3)
 
     loads[1].wait()
     loads[2].wait()
@@ -209,26 +227,17 @@
             def _():
                 stat[my_rows] = source[s]
 
-    ring_e = RingReduce(w, acc_e, pass_e, came_e, x, to_x)
-    ring_f = RingReduce(w, acc_f, pass_f, came_f, x, to_x)
-    core_e.wait_recv()
-    for k in range(NK):
-        acc_e[k] = total(gv[order[OWNERS + k], pl.ds(c * HALF, HALF)], recv_e[k])
-    ring_e.send_far()
-    ring_e.send_right()
-    ring_e.send_left()
-
     def add_f(step):
         at = (x + turns[step]) % NX
         core_f[step].wait_recv()
         for q in range(NZ):
-            acc_f[at * NZ + q] = total(gv[order[(at * NZ + q) * NC + c]], recv_f[at * NZ + q])
+            acc_f[at * NZ + q] = total(gv[table[(at * NZ + q) * NC + c]], recv_f[at * NZ + q])
 
     add_f(0)
+    ring_e.forward()
     ring_f.send_far()
     add_f(1)
     ring_f.send_right()
-    ring_e.forward()
     add_f(2)
     ring_f.send_left()
     add_f(3)
@@ -284,15 +293,22 @@
     for copy in ext_core:
         copy.wait_recv()
     for s in range(1, SLOTS):
-        own[s] = ext[extra_of[s]]
+        own[s] = ext[table[EXTRA_OF + s]]
         send_g(s)
+
+    stores = []
+
+    def store(src, dst):
+        copy = pltpu.make_async_copy(src, dst, store_sem.at[len(stores)])
+        copy.start()
+        stores.append(copy)
 
     loads[3].wait()
     loads[4].wait()
     n_send, n_recv = w.take(SLOTS), w.take(NM)
     n_copies = []
     for s in range(SLOTS):
-        held = jnp.full((ROWS, COLS), occupied[s]) > 0
+        held = jnp.full((ROWS, COLS), table[OCCUPIED + s]) > 0
         g = own[s].astype(F32)
         m = 0.9 * fv[s] + 0.1 * g
         v = 0.95 * sv[s] + 0.05 * g * g
@@ -314,6 +330,8 @@
         def _():
             norms_in[j] = norms[s]
 
+    store(first_out, first_hbm)
+    store(second_out, second_hbm)
     handed = [
         w.make(grad.at[pl.ds(i * ROWS, ROWS)], grad.at[pl.ds(i * ROWS, ROWS)], core, g_core + i, g_core + i)
         for i in range(NM)
@@ -459,47 +477,43 @@
         return RingGather(w, part, x, to_x)
 
     rings = {k: ring_of(k) for k in range(NZ)}
-    rings[0].start()
-    for s in range(1, SLOTS):
-        wait_update(s)
+    for q in range(1, SLOTS):
+        wait_update(q)
 
     def picked(e, which):
-        at = mine_of[e]
+        at = table[MINE_OF + e]
         value = update[at, pl.ds(which * HALF, HALF)]
         return jnp.where(jnp.full(value.shape, at) > 0, value.astype(F32), 0.0)
 
     for e in range(EXTRAS):
         send_d[e] = picked(e, other).astype(BF16)
     core_d = w.go(send_d, recv_d, core)
+    ring_d = RingReduce(w, acc_d, pass_d, came_d, x, to_x)
     core_d.wait_recv()
-    ring_d = RingReduce(w, acc_d, pass_d, came_d, x, to_x)
-    for k in turns:
+    for k, send in ((2, ring_d.send_far), (1, ring_d.send_right), (3, ring_d.send_left), (0, None)):
         for q in range(NZ):
             e = ((x + k) % NX) * NZ + q
             acc_d[e] = (picked(e, c) + recv_d[e].astype(F32)).astype(BF16)
-        if k == 2:
-            ring_d.send_far()
-        if k == 1:
-            ring_d.send_right()
-        if k == 3:
-            ring_d.send_left()
+        if send:
+            send()
+    ring_d.forward()
+    rings[0].start()
+    ring_d.finish(sum_d)
+    z_d = [w.go(sum_d.at[(z + k) % NZ], from_z_d.at[k - 1], dp_of(x, (z + k) % NZ, c)) for k in FAR_FIRST]
     for copy, k in sorted(zip(f_z, FAR_FIRST), key=lambda pair: pair[1] == 2):
         copy.wait_recv()
         rings[k].start()
     f_line = lambda at: all_of.at[pl.ds(c * NK + at * NZ, NZ)]
     f_core = [w.go(f_line(x), f_line(x), core)]
-    ring_d.forward()
     rings[0].forward()
-    ring_d.finish(sum_d)
-    z_d = [w.go(sum_d.at[(z + k) % NZ], from_z_d.at[k - 1], dp_of(x, (z + k) % NZ, c)) for k in FAR_FIRST]
-    for k in (1, 3, 2):
-        rings[k].forward()
     for copy in z_d:
         copy.wait_recv()
     here_e = (OWNERS + x * NZ + z, pl.ds(c * HALF, HALF))
     all_of[here_e] = total(sum_d[z], from_z_d[0], from_z_d[1], from_z_d[2])
     mine = all_of.at[here_e]
     z_g = [w.go(mine, mine, dp_of(x, (z + k) % NZ, c)) for k in FAR_FIRST]
+    for k in (1, 3, 2):
+        rings[k].forward()
 
     for role in range(2):
         for s in range(SLOTS):
@@ -511,9 +525,11 @@
                 ).wait_recv()
 
             old, new = ((lv, left_out), (rv, right_out))[role]
-            held = jnp.full((ROWS, COLS), occupied[s]) > 0
+            held = jnp.full((ROWS, COLS), table[OCCUPIED + s]) > 0
             new[s] = jnp.where(held, 0.9 * old[s] + 0.1 * terms[role, s].astype(F32), old[s])
 
+    store(left_out, left_hbm)
+    store(right_out, right_hbm)
     for copy in z_g:
         copy.wait_recv()
     e_core = spread(all_of, OWNERS)
@@ -524,11 +540,17 @@
     for k in range(NZ):
         rings[k].finish_far()
     f_core.append(w.go(f_line((x + 2) % NX), f_line((x + 2) % NX), core))
-    for copy in f_core + e_core:
-        copy.wait_recv()
-    for b in range(BLOCKS):
-        out[b] = all_of[place_of[b]]
-
+    for copy in f_core:
+        copy.wait_recv()
+    firsts = pl.ds(0, OWNERS)
+    store(all_of.at[firsts], all_out.at[firsts])
+    for copy in e_core:
+        copy.wait_recv()
+    extras = pl.ds(OWNERS, EXTRAS)
+    store(all_of.at[extras], all_out.at[extras])
+
+    for copy in stores:
+        copy.wait()
     for copy in w.sent:
         copy.wait_send()
     for here, copy in stat_copies + n_copies + t_copies:
@@ -562,7 +584,7 @@
                 d_copies[i].wait_send()
 
 
-def whole_step(order, place_of, occupied, extra_of, mine_of, grads, left, right, first, second):
+def whole_step(table, grads, left, right, first, second):
     state = jax.ShapeDtypeStruct((SLOTS, ROWS, COLS), F32)
     v = lambda *shape, kind=BF16: pltpu.VMEM(shape, kind)
     dma = pltpu.SemaphoreType.DMA
@@ -571,9 +593,11 @@
     return pl.pallas_call(
         kernel,
         out_shape=(jax.ShapeDtypeStruct((BLOCKS, ROWS, COLS), BF16), state, state, state, state),
-        in_specs=[SMEM] * 5 + [ANY] * 5,
-        out_specs=(VMEM,) * 5,
+        in_specs=[SMEM] + [ANY] * 5,
+        out_specs=(ANY,) * 5,
         scratch_shapes=[v(BLOCKS, *full)]
+        + [v(SLOTS, *full, kind=F32)] * 4
+        + [v(BLOCKS, *full)]
         + [v(SLOTS, *full, kind=F32)] * 4
         + [
             v(NK, *full), v(NK, *half), v(NK, *full), v(NK, *half), v(NK, *full), v(NK, *half),
@@ -587,44 +611,95 @@
         + [v(ORDER, COLS)] * 7
         + [v(SLOTS, *full)]
         + [
-            v(BLOCKS, *full), v(EXTRAS, *half), v(EXTRAS, *half), v(EXTRAS, *half), v(2, 2, *half),
+            v(EXTRAS, *half), v(EXTRAS, *half), v(EXTRAS, *half), v(2, 2, *half),
             v(2, NZ, *half), v(NZ, *half), v(3, *half),
         ]
-        + [dma((SEMS,)), dma((SEMS,)), dma((5,)), dma((1,))],
+        + [dma((SEMS,)), dma((SEMS,)), dma((5,)), dma((7,))],
         compiler_params=pltpu.CompilerParams(
             collective_id=0, has_side_effects=True, vmem_limit_bytes=56 << 20
         ),
         name="shampoo_step",
-    )(order, place_of, occupied, extra_of, mine_of, grads, left, right, first, second)
+    )(table, grads, left, right, first, second)
+
+
+def table_kernel(owner, table, counts):
+    me = lax.axis_index("dp")
+
+    def clear(i, carry):
+        table[i] = 0
+        return carry
+
+    def clear_counts(i, carry):
+        counts[i] = 0
+        return carry
+
+    lax.fori_loop(OCCUPIED, MINE_OF + EXTRAS, clear, 0)
+    lax.fori_loop(0, OWNERS, clear_counts, 0)
+
+    def visit(b, rank):
+        o = owner[b]
+        slot = counts[o]
+        counts[o] = slot + 1
+        again = slot > 0
+        table[jnp.where(again, OWNERS + rank, o)] = b
+        table[PLACE_OF + b] = jnp.where(again, OWNERS + rank, (o % NC) * NK + o // NC)
+
+        @pl.when(o == me)
+        def _():
+            table[OCCUPIED + slot] = 1
+
+            @pl.when(again)
+            def _():
+                table[EXTRA_OF + slot] = rank
+                table[MINE_OF + rank] = slot
+
+        return rank + again.astype(jnp.int32)
+
+    lax.fori_loop(0, BLOCKS, visit, jnp.int32(0))
 
 
 def tables(owners):
-    owner = owners[:, 0]
-    me = lax.axis_index("dp")
-    spots = jnp.arange(BLOCKS, dtype=jnp.int32)
-    earlier = spots[None, :] < spots[:, None]
-    slot = jnp.sum((owner[:, None] == owner[None, :]) & earlier, axis=1, dtype=jnp.int32)
-    again = slot > 0
-    rank = jnp.sum(again[None, :] & earlier, axis=1, dtype=jnp.int32)
-    sorted_at = jnp.where(again, OWNERS + rank, owner)
-    order = jnp.sum(jnp.where(sorted_at[None, :] == spots[:, None], spots[None, :], 0), axis=1)
-    place_of = jnp.where(again, OWNERS + rank, (owner % NC) * NK + owner // NC)
-    mine = owner == me
-    slots = jnp.arange(SLOTS, dtype=jnp.int32)
-    holds = mine[None, :] & (slot[None, :] == slots[:, None])
-    occupied = jnp.sum(holds, axis=1, dtype=jnp.int32)
-    extra_of = jnp.sum(jnp.where(holds & again[None, :], rank[None, :], 0), axis=1)
-    extras = jnp.arange(EXTRAS, dtype=jnp.int32)
-    held = (mine & again)[None, :] & (rank[None, :] == extras[:, None])
-    mine_of = jnp.sum(jnp.where(held, slot[None, :], 0), axis=1)
-    return order, place_of, occupied, extra_of, mine_of
+    return pl.pallas_call(
+        table_kernel,
+        out_shape=jax.ShapeDtypeStruct((TABLE,), jnp.int32),
+        in_specs=[SMEM],
+        out_specs=SMEM,
+        scratch_shapes=[pltpu.SMEM((OWNERS,), jnp.int32)],
+        name="tables",
+    )(owners[:, 0])
+
+
+def output_kernel(table, all_of, a, b, c, d, out, a_out, b_out, c_out, d_out, sems):
+    copies = [
+        pltpu.make_async_copy(src, dst.at[0], sems.at[BLOCKS + i])
+        for i, (src, dst) in enumerate(((a, a_out), (b, b_out), (c, c_out), (d, d_out)))
+    ]
+    copies += [
+        pltpu.make_async_copy(all_of.at[table[PLACE_OF + i]], out.at[i], sems.at[i]) for i in range(BLOCKS)
+    ]
+    for copy in copies:
+        copy.start()
+    for copy in copies:
+        copy.wait()
+
+
+def outputs(table, *parts):
+    state = jax.ShapeDtypeStruct((1, SLOTS, ROWS, COLS), F32)
+    return pl.pallas_call(
+        output_kernel,
+        out_shape=(jax.ShapeDtypeStruct((BLOCKS, ROWS, COLS), BF16), state, state, state, state),
+        in_specs=[SMEM] + [ANY] * 5,
+        out_specs=(ANY,) * 5,
+        scratch_shapes=[pltpu.SemaphoreType.DMA((BLOCKS + 4,))],
+        compiler_params=pltpu.CompilerParams(vmem_limit_bytes=56 << 20),
+        name="outputs",
+    )(table, *parts)
 
 
 def body(grads, owners, left_stat, right_stat, first_moment, second_moment):
-    direction, *states = whole_step(
-        *tables(owners), grads[0], left_stat[0], right_stat[0], first_moment[0], second_moment[0]
-    )
-    return (direction, *(state[None] for state in states))
+    table = tables(owners)
+    parts = whole_step(table, grads[0], left_stat[0], right_stat[0], first_moment[0], second_moment[0])
+    return outputs(table, *parts)
 
 
 def solution(mesh):

time: 123 us -> 273 us (2.22)
  Pallas kernels: 108 us -> 272 us
  local copies, waits for them, and re-layouts: 7.21 us -> 0 us
  other arithmetic: 4.8 us -> 0 us
    pallas_call x0 -> x2, Pallas kernels: none -> 164 us  [the longest x1 161 us: outputs(): pl.pallas_call(output_kernel, out_shape=(jax.ShapeDtypeStruct((BLOCKS, RO...]
    unnamed x13 -> x0, local copies, waits for them, and re-layouts: 7.21 us -> none
    reduce_sum x5 -> x0, other arithmetic: 2.95 us -> none  [the longest x1 0.91 us: tables(): jnp.sum((owner[:, None] == owner[None, :]) & earlier, axis=1, dtype=jnp.i...]
where the time goes in v3:
time: 273 us
  Pallas kernels  272 us (100%)
    pallas_call x1, Pallas kernels, outputs(): pl.pallas_call(output_kernel, out_shape=(jax.ShapeDtypeStruct((BLOCKS, RO...  161 us
    pallas_call x1, Pallas kernels, whole_step(): pl.pallas_call(kernel, out_shape=(jax.ShapeDtypeStruct((BLOCKS, ROWS, COL...  109 us

profile of v3, /device:TPU:25, one launch (start us, length us, event | category | flops | bytes accessed | tf_op | source)
XLA Modules:
  0.0 273.1 jit_solution(16691562007635449527)
XLA Ops:
  0.6 2.5 tables.1.table
  3.1 108.9 %shampoo_step.1 = (bf16[48,64,512]{2,1,0:T(8,128)(2,1)}, f32[4,64,512]{2,1,0:T(8,128)}, f32[4,64,512]{2,1,0:T(8,128)}, f32[4,64,512]{2,1,0:T(8,128)}, f32[4,64,512]{2,1,0:T(8,128)}) custom-call(s32[128]{0:T(128)} %tables.1.table, bf16[48,64,512]{2,1,0:T(8,128)(2,1)} %bitcast.6, f32[4,64,512]{2,1,0:T(8,128)} %bitcast.7, f32[4,64,512]{2,1,0:T(8,128)} %bitcast.8, ...), custom_call_target="tpu_custom_call" | custom-call | tf_op jit(solution)/shard_map/shampoo_step/pallas_call | solution.py:593
  112.1 161.1 %outputs.1 = (bf16[48,64,512]{2,1,0:T(8,128)(2,1)}, f32[1,4,64,512]{3,2,1,0:T(8,128)}, f32[1,4,64,512]{3,2,1,0:T(8,128)}, f32[1,4,64,512]{3,2,1,0:T(8,128)}, f32[1,4,64,512]{3,2,1,0:T(8,128)}) custom-call(s32[128]{0:T(128)} %tables.1.table, bf16[48,64,512]{2,1,0:T(8,128)(2,1)} %get-tuple-element.10.all_of, f32[4,64,512]{2,1,0:T(8,128)} %get-tuple-element.11.a, ...), custom_call_target="tpu_custom_call" | custom-call | tf_op jit(solution)/shard_map/outputs/pallas_call | solution.py:688

commit v4 on v3

--- a/solution.py
+++ b/solution.py
@@ -20,7 +20,7 @@
 OWNERS = NK * NC
 EXTRAS = BLOCKS - OWNERS
 FAR_FIRST = (2, 1, 3)
-SEMS = 192
+SEMS = 256
 PLACE_OF, OCCUPIED, EXTRA_OF, MINE_OF, TABLE = 48, 96, 100, 104, 128
 
 
@@ -176,6 +176,26 @@
                 greeted += 1
     pl.semaphore_wait(barrier, greeted)
 
+    stat_send, stat_recv = w.take(2 * SLOTS), w.take(NM)
+    stat_copies = []
+    for s in range(SLOTS):
+        for role, source in enumerate((left, right)):
+            copy = w.make(
+                source.at[s], stat.at[my_rows], device_of(x, z, role, 2 * s + c), stat_send + 2 * s + role,
+                stat_recv + j,
+            )
+            here = (c == role) & (j == 2 * s + c)
+            stat_copies.append((here, copy))
+
+    def send_stats(slots):
+        for here, copy in [stat_copies[2 * s + role] for s in slots for role in range(NC)]:
+
+            @pl.when(jnp.logical_not(here))
+            def _():
+                copy.start()
+
+    send_stats((0, 1))
+
     loads[0].wait()
     for k in range(NK):
         send_e[k] = gv[table[OWNERS + k], pl.ds(other * HALF, HALF)]
@@ -206,32 +226,20 @@
     ring_e.send_left()
     add_e(3)
 
-    loads[1].wait()
-    loads[2].wait()
-    stat_send, stat_recv = w.take(2 * SLOTS), w.take(NM)
-    stat_copies = []
-    for s in range(SLOTS):
-        for role, source in enumerate((lv, rv)):
-            copy = w.make(
-                source.at[s], stat.at[my_rows], device_of(x, z, role, 2 * s + c), stat_send + 2 * s + role,
-                stat_recv + j,
-            )
-            here = (c == role) & (j == 2 * s + c)
-            stat_copies.append((here, copy))
-
-            @pl.when(jnp.logical_not(here))
-            def _():
-                copy.start()
-
-            @pl.when(here)
-            def _():
-                stat[my_rows] = source[s]
-
     def add_f(step):
         at = (x + turns[step]) % NX
         core_f[step].wait_recv()
         for q in range(NZ):
             acc_f[at * NZ + q] = total(gv[table[(at * NZ + q) * NC + c]], recv_f[at * NZ + q])
+
+    loads[1].wait()
+    loads[2].wait()
+    for s in range(SLOTS):
+        for role, source in enumerate((lv, rv)):
+
+            @pl.when((c == role) & (j == 2 * s + c))
+            def _():
+                stat[my_rows] = source[s]
 
     add_f(0)
     ring_e.forward()
@@ -249,27 +257,41 @@
     mine = ext.at[x * NZ + z, pl.ds(c * HALF, HALF)]
     ext[x * NZ + z, pl.ds(c * HALF, HALF)] = total(sum_e[z], from_z_e[0], from_z_e[1], from_z_e[2])
     z_g = [w.go(mine, mine, dp_of(x, (z + k) % NZ, c)) for k in FAR_FIRST]
+
+    def spread(ref, base, zs):
+        def ring_of(k):
+            at_z = (z + NZ - k) % NZ
+            part = lambda at, h: ref.at[base + at * NZ + at_z, pl.ds(c * HALF + h * 16, 16)]
+            return RingGather(w, part, x, to_x)
+
+        line = lambda at: ref.at[pl.ds(base + at * NZ, NZ), pl.ds(c * HALF, HALF)]
+        rings = {k: ring_of(k) for k in range(NZ)}
+        rings[0].start()
+
+        def rest(meanwhile):
+            for k in (1, 3, 2):
+                zs[FAR_FIRST.index(k)].wait_recv()
+                rings[k].start()
+            across = [w.go(line(x), line(x), core)]
+            meanwhile()
+            for k in (0, 1, 3, 2):
+                rings[k].forward()
+            for k in range(NZ):
+                rings[k].finish_near()
+            for at in ((x + 3) % NX, (x + 1) % NX):
+                across.append(w.go(line(at), line(at), core))
+            for k in range(NZ):
+                rings[k].finish_far()
+            far = (x + 2) % NX
+            across.append(w.go(line(far), line(far), core))
+            return across
+
+        return rest
+
+    spread_rest = spread(ext, 0, z_g)
     ring_f.finish(sum_f)
     z_f = [w.go(sum_f.at[(z + k) % NZ], from_z_f.at[k - 1], dp_of(x, (z + k) % NZ, c)) for k in FAR_FIRST]
-    for copy in z_g:
-        copy.wait_recv()
-
-    def spread(ref, base):
-        part = lambda at, h: ref.at[pl.ds(base + at * NZ + 2 * h, 2), pl.ds(c * HALF, HALF)]
-        line = lambda at: ref.at[pl.ds(base + at * NZ, NZ), pl.ds(c * HALF, HALF)]
-        ring = RingGather(w, part, x, to_x)
-        ring.start()
-        across = [w.go(line(x), line(x), core)]
-        ring.forward()
-        ring.finish_near()
-        for at in (ring.left, ring.right):
-            across.append(w.go(line(at), line(at), core))
-        ring.finish_far()
-        far = (x + 2) % NX
-        across.append(w.go(line(far), line(far), core))
-        return across
-
-    ext_core = spread(ext, 0)
+    ext_core = spread_rest(lambda: send_stats((2, 3)))
     for copy in z_f:
         copy.wait_recv()
     own[0] = total(sum_f[z], from_z_f[0], from_z_f[1], from_z_f[2])
@@ -512,6 +534,7 @@
     all_of[here_e] = total(sum_d[z], from_z_d[0], from_z_d[1], from_z_d[2])
     mine = all_of.at[here_e]
     z_g = [w.go(mine, mine, dp_of(x, (z + k) % NZ, c)) for k in FAR_FIRST]
+    spread_rest = spread(all_of, OWNERS, z_g)
     for k in (1, 3, 2):
         rings[k].forward()
 
@@ -530,13 +553,11 @@
 
     store(left_out, left_hbm)
     store(right_out, right_hbm)
-    for copy in z_g:
-        copy.wait_recv()
-    e_core = spread(all_of, OWNERS)
     for k in range(NZ):
         rings[k].finish_near()
     for at in ((x + 3) % NX, (x + 1) % NX):
         f_core.append(w.go(f_line(at), f_line(at), core))
+    e_core = spread_rest(lambda: None)
     for k in range(NZ):
         rings[k].finish_far()
     f_core.append(w.go(f_line((x + 2) % NX), f_line((x + 2) % NX), core))
@@ -669,17 +690,24 @@
     )(owners[:, 0])
 
 
-def output_kernel(table, all_of, a, b, c, d, out, a_out, b_out, c_out, d_out, sems):
-    copies = [
-        pltpu.make_async_copy(src, dst.at[0], sems.at[BLOCKS + i])
-        for i, (src, dst) in enumerate(((a, a_out), (b, b_out), (c, c_out), (d, d_out)))
-    ]
-    copies += [
-        pltpu.make_async_copy(all_of.at[table[PLACE_OF + i]], out.at[i], sems.at[i]) for i in range(BLOCKS)
-    ]
-    for copy in copies:
+def output_kernel(
+    table, all_of, a, b, c, d, out, a_out, b_out, c_out, d_out, held, a_held, b_held, c_held, d_held, came, sent
+):
+    load = pltpu.make_async_copy(all_of, held, came.at[0])
+    load.start()
+    states = ((a, a_held, a_out), (b, b_held, b_out), (c, c_held, c_out), (d, d_held, d_out))
+    ins = [pltpu.make_async_copy(src, mid, came.at[1 + i]) for i, (src, mid, _) in enumerate(states)]
+    outs = [pltpu.make_async_copy(mid, dst.at[0], sent.at[1 + i]) for i, (_, mid, dst) in enumerate(states)]
+    for copy in ins:
         copy.start()
-    for copy in copies:
+    load.wait()
+    for i in range(BLOCKS):
+        pltpu.make_async_copy(held.at[table[PLACE_OF + i]], out.at[i], sent.at[0]).start()
+    for copy_in, copy_out in zip(ins, outs):
+        copy_in.wait()
+        copy_out.start()
+    pltpu.make_async_copy(held, out, sent.at[0]).wait()
+    for copy in outs:
         copy.wait()
 
 
@@ -690,7 +718,9 @@
         out_shape=(jax.ShapeDtypeStruct((BLOCKS, ROWS, COLS), BF16), state, state, state, state),
         in_specs=[SMEM] + [ANY] * 5,
         out_specs=(ANY,) * 5,
-        scratch_shapes=[pltpu.SemaphoreType.DMA((BLOCKS + 4,))],
+        scratch_shapes=[pltpu.VMEM((BLOCKS, ROWS, COLS), BF16)]
+        + [pltpu.VMEM((SLOTS, ROWS, COLS), F32)] * 4
+        + [pltpu.SemaphoreType.DMA((5,))] * 2,
         compiler_params=pltpu.CompilerParams(vmem_limit_bytes=56 << 20),
         name="outputs",
     )(table, *parts)

time: 273 us -> 109 us (0.40)
  Pallas kernels: 272 us -> 108 us
    pallas_call x1, Pallas kernels: 161 us -> 4.95 us  [outputs(): pl.pallas_call(output_kernel, out_shape=(jax.ShapeDtypeStruct((BLOCKS, RO...]
    pallas_call x1, Pallas kernels: 109 us -> 101 us  [whole_step(): pl.pallas_call(kernel, out_shape=(jax.ShapeDtypeStruct((BLOCKS, ROWS, COL...]
where the time goes in v4:
time: 109 us
  Pallas kernels  108 us (99%)
    pallas_call x1, Pallas kernels, whole_step(): pl.pallas_call(kernel, out_shape=(jax.ShapeDtypeStruct((BLOCKS, ROWS, COL...  101 us
    pallas_call x1, Pallas kernels, outputs(): pl.pallas_call(output_kernel, out_shape=(jax.ShapeDtypeStruct((BLOCKS, RO...  4.95 us
    pallas_call x1, Pallas kernels, tables(): pl.pallas_call(table_kernel, out_shape=jax.ShapeDtypeStruct((TABLE,), jnp...  2.47 us

profile of v4, /device:TPU:25, one launch (start us, length us, event | category | flops | bytes accessed | tf_op | source)
XLA Modules:
  0.0 109.0 jit_solution(10426750231351254626)
XLA Ops:
  0.6 2.5 %tables.1.table = s32[128]{0:T(128)} custom-call(s32[48]{0:T(128)} %bitcast.11), custom_call_target="tpu_custom_call" | custom-call | tf_op jit(solution)/shard_map/tables/pallas_call | solution.py:683
  3.1 101.0 %shampoo_step.1 = (bf16[48,64,512]{2,1,0:T(8,128)(2,1)}, f32[4,64,512]{2,1,0:T(8,128)}, f32[4,64,512]{2,1,0:T(8,128)}, f32[4,64,512]{2,1,0:T(8,128)}, f32[4,64,512]{2,1,0:T(8,128)}) custom-call(s32[128]{0:T(128)} %tables.1.table, bf16[48,64,512]{2,1,0:T(8,128)(2,1)} %bitcast.6, f32[4,64,512]{2,1,0:T(8,128)} %bitcast.7, f32[4,64,512]{2,1,0:T(8,128)} %bitcast.8, ...), custom_call_target="tpu_custom_call" | custom-call | tf_op jit(solution)/shard_map/shampoo_step/pallas_call | solution.py:614
  104.1 4.9 %outputs.1 = (bf16[48,64,512]{2,1,0:T(8,128)(2,1)}, f32[1,4,64,512]{3,2,1,0:T(8,128)}, f32[1,4,64,512]{3,2,1,0:T(8,128)}, f32[1,4,64,512]{3,2,1,0:T(8,128)}, f32[1,4,64,512]{3,2,1,0:T(8,128)}) custom-call(s32[128]{0:T(128)} %tables.1.table, bf16[48,64,512]{2,1,0:T(8,128)(2,1)} %get-tuple-element.10.all_of, f32[4,64,512]{2,1,0:T(8,128)} %get-tuple-element.11.a, ...), custom_call_target="tpu_custom_call" | custom-call | tf_op jit(solution)/shard_map/outputs/pallas_call | solution.py:716

commit v5 on v4

--- a/solution.py
+++ b/solution.py
@@ -290,8 +290,14 @@
 
     spread_rest = spread(ext, 0, z_g)
     ring_f.finish(sum_f)
-    z_f = [w.go(sum_f.at[(z + k) % NZ], from_z_f.at[k - 1], dp_of(x, (z + k) % NZ, c)) for k in FAR_FIRST]
-    ext_core = spread_rest(lambda: send_stats((2, 3)))
+    z_f = []
+    def then():
+        for k in FAR_FIRST:
+            at = (z + k) % NZ
+            z_f.append(w.go(sum_f.at[at], from_z_f.at[k - 1], dp_of(x, at, c)))
+        send_stats((2, 3))
+
+    ext_core = spread_rest(then)
     for copy in z_f:
         copy.wait_recv()
     own[0] = total(sum_f[z], from_z_f[0], from_z_f[1], from_z_f[2])

time: 109 us -> 109 us (level)
  no operation moved by 1% of the time
where the time goes in v5:
time: 109 us; the launch traced here: 108 us
  Pallas kernels  108 us (99%)
    pallas_call x1, Pallas kernels, whole_step(): pl.pallas_call(kernel, out_shape=(jax.ShapeDtypeStruct((BLOCKS, ROWS, COL...  100 us
    pallas_call x1, Pallas kernels, outputs(): pl.pallas_call(output_kernel, out_shape=(jax.ShapeDtypeStruct((BLOCKS, RO...  4.95 us
    pallas_call x1, Pallas kernels, tables(): pl.pallas_call(table_kernel, out_shape=jax.ShapeDtypeStruct((TABLE,), jnp...  2.47 us

profile of v5, /device:TPU:25, one launch (start us, length us, event | category | flops | bytes accessed | tf_op | source)
XLA Modules:
  0.0 108.3 jit_solution(7374484615181036424)
XLA Ops:
  0.6 2.5 %tables.1.table = s32[128]{0:T(128)} custom-call(s32[48]{0:T(128)} %bitcast.11), custom_call_target="tpu_custom_call" | custom-call | tf_op jit(solution)/shard_map/tables/pallas_call | solution.py:689
  3.1 100.2 %shampoo_step.1 = (bf16[48,64,512]{2,1,0:T(8,128)(2,1)}, f32[4,64,512]{2,1,0:T(8,128)}, f32[4,64,512]{2,1,0:T(8,128)}, f32[4,64,512]{2,1,0:T(8,128)}, f32[4,64,512]{2,1,0:T(8,128)}) custom-call(s32[128]{0:T(128)} %tables.1.table, bf16[48,64,512]{2,1,0:T(8,128)(2,1)} %bitcast.6, f32[4,64,512]{2,1,0:T(8,128)} %bitcast.7, f32[4,64,512]{2,1,0:T(8,128)} %bitcast.8, ...), custom_call_target="tpu_custom_call" | custom-call | tf_op jit(solution)/shard_map/shampoo_step/pallas_call | solution.py:620
  103.3 4.9 %outputs.1 = (bf16[48,64,512]{2,1,0:T(8,128)(2,1)}, f32[1,4,64,512]{3,2,1,0:T(8,128)}, f32[1,4,64,512]{3,2,1,0:T(8,128)}, f32[1,4,64,512]{3,2,1,0:T(8,128)}, f32[1,4,64,512]{3,2,1,0:T(8,128)}) custom-call(s32[128]{0:T(128)} %tables.1.table, bf16[48,64,512]{2,1,0:T(8,128)(2,1)} %get-tuple-element.10.all_of, f32[4,64,512]{2,1,0:T(8,128)} %get-tuple-element.11.a, ...), custom_call_target="tpu_custom_call" | custom-call | tf_op jit(solution)/shard_map/outputs/pallas_call | solution.py:722

commit v6 on v4

--- a/solution.py
+++ b/solution.py
@@ -187,14 +187,14 @@
             here = (c == role) & (j == 2 * s + c)
             stat_copies.append((here, copy))
 
-    def send_stats(slots):
-        for here, copy in [stat_copies[2 * s + role] for s in slots for role in range(NC)]:
+    def send_stats(role):
+        for here, copy in stat_copies[role::NC]:
 
             @pl.when(jnp.logical_not(here))
             def _():
                 copy.start()
 
-    send_stats((0, 1))
+    send_stats(0)
 
     loads[0].wait()
     for k in range(NK):
@@ -291,7 +291,7 @@
     spread_rest = spread(ext, 0, z_g)
     ring_f.finish(sum_f)
     z_f = [w.go(sum_f.at[(z + k) % NZ], from_z_f.at[k - 1], dp_of(x, (z + k) % NZ, c)) for k in FAR_FIRST]
-    ext_core = spread_rest(lambda: send_stats((2, 3)))
+    ext_core = spread_rest(lambda: send_stats(1))
     for copy in z_f:
         copy.wait_recv()
     own[0] = total(sum_f[z], from_z_f[0], from_z_f[1], from_z_f[2])

time: 109 us -> 107 us (0.982); the launches traced: 109 us -> 105 us
  Pallas kernels: 108 us -> 105 us
    pallas_call x1, Pallas kernels: 101 us -> 97.4 us  [whole_step(): pl.pallas_call(kernel, out_shape=(jax.ShapeDtypeStruct((BLOCKS, ROWS, COL...]
where the time goes in v6:
time: 107 us; the launch traced here: 105 us
  Pallas kernels  105 us (98%)
    pallas_call x1, Pallas kernels, whole_step(): pl.pallas_call(kernel, out_shape=(jax.ShapeDtypeStruct((BLOCKS, ROWS, COL...  97.4 us
    pallas_call x1, Pallas kernels, outputs(): pl.pallas_call(output_kernel, out_shape=(jax.ShapeDtypeStruct((BLOCKS, RO...  4.95 us
    pallas_call x1, Pallas kernels, tables(): pl.pallas_call(table_kernel, out_shape=jax.ShapeDtypeStruct((TABLE,), jnp...  2.47 us

profile of v6, /device:TPU:25, one launch (start us, length us, event | category | flops | bytes accessed | tf_op | source)
XLA Modules:
  0.0 105.5 jit_solution(11281706059818995779)
XLA Ops:
  0.6 2.5 %tables.1.table = s32[128]{0:T(128)} custom-call(s32[48]{0:T(128)} %bitcast.11), custom_call_target="tpu_custom_call" | custom-call | tf_op jit(solution)/shard_map/tables/pallas_call | solution.py:683
  3.1 97.4 %shampoo_step.1 = (bf16[48,64,512]{2,1,0:T(8,128)(2,1)}, f32[4,64,512]{2,1,0:T(8,128)}, f32[4,64,512]{2,1,0:T(8,128)}, f32[4,64,512]{2,1,0:T(8,128)}, f32[4,64,512]{2,1,0:T(8,128)}) custom-call(s32[128]{0:T(128)} %tables.1.table, bf16[48,64,512]{2,1,0:T(8,128)(2,1)} %bitcast.6, f32[4,64,512]{2,1,0:T(8,128)} %bitcast.7, f32[4,64,512]{2,1,0:T(8,128)} %bitcast.8, ...), custom_call_target="tpu_custom_call" | custom-call | tf_op jit(solution)/shard_map/shampoo_step/pallas_call | solution.py:614
  100.5 4.9 %outputs.1 = (bf16[48,64,512]{2,1,0:T(8,128)(2,1)}, f32[1,4,64,512]{3,2,1,0:T(8,128)}, f32[1,4,64,512]{3,2,1,0:T(8,128)}, f32[1,4,64,512]{3,2,1,0:T(8,128)}, f32[1,4,64,512]{3,2,1,0:T(8,128)}) custom-call(s32[128]{0:T(128)} %tables.1.table, bf16[48,64,512]{2,1,0:T(8,128)(2,1)} %get-tuple-element.10.all_of, f32[4,64,512]{2,1,0:T(8,128)} %get-tuple-element.11.a, ...), custom_call_target="tpu_custom_call" | custom-call | tf_op jit(solution)/shard_map/outputs/pallas_call | solution.py:716
